TPU v7x, 32 devices: a whole 2x2x4 slice. The times are simulated.
32 devices in a mesh: dp: 8 (over y, x, core), mp: 4 (over z).
Axes of the slice: x: 2, y: 2, z: 4, core: 2. Of those that a mesh axis runs over, the one named last changes fastest.
Arguments:
- qkv_weight: float32 [2, 3, 768, 768], P(None, None, 'dp', 'mp'), may hold values from -0.21875 to 0.21875
- qkv_first: float32 [2, 3, 768, 768], P(None, None, 'dp', 'mp'), may hold values from -2.861023e-06 to 2.861023e-06
- qkv_second: float32 [2, 3, 768, 768], P(None, None, 'dp', 'mp'), may hold values from 2.001037e-13 to 3.1723758e-12
- out_weight: float32 [2, 768, 768], P(None, 'mp', 'dp'), may hold values from -0.875 to 0.875
- out_first: float32 [2, 768, 768], P(None, 'mp', 'dp'), may hold values from -2.861023e-06 to 2.861023e-06
- out_second: float32 [2, 768, 768], P(None, 'mp', 'dp'), may hold values from 2.001037e-13 to 3.1723758e-12
- up_weight: float32 [2, 768, 3072], P(None, 'dp', 'mp'), may hold values from -0.21875 to 0.21875
- up_first: float32 [2, 768, 3072], P(None, 'dp', 'mp'), may hold values from -2.861023e-06 to 2.861023e-06
- up_second: float32 [2, 768, 3072], P(None, 'dp', 'mp'), may hold values from 2.001037e-13 to 3.1723758e-12
- down_weight: float32 [2, 3072, 768], P(None, 'mp', 'dp'), may hold values from -0.109375 to 0.109375
- down_first: float32 [2, 3072, 768], P(None, 'mp', 'dp'), may hold values from -2.861023e-06 to 2.861023e-06
- down_second: float32 [2, 3072, 768], P(None, 'mp', 'dp'), may hold values from 2.001037e-13 to 3.1723758e-12
- code_table: float32 [8192, 768], P('mp', 'dp')
- table_first: float32 [8192, 768], P('mp', 'dp'), may hold values from -2.861023e-06 to 2.861023e-06
- table_second: float32 [8192, 768], P('mp', 'dp'), may hold values from 2.001037e-13 to 3.1723758e-12
- small_params: float32 [42144], replicated
- small_first: float32 [42144], replicated, may hold values from -2.861023e-06 to 2.861023e-06
- small_second: float32 [42144], replicated, may hold values from 2.001037e-13 to 3.1723758e-12
- patch_codes: int32 [64, 196], P('dp'), may hold values from 0 to 8191
- masked_pos: int32 [64, 75], P('dp'), may hold values from 0 to 195, as said below
- masked_count: int32 [64], P('dp'), may hold values from 1 to 75, as said below
Outputs:
- qkv_weight_new: float32 [2, 3, 768, 768], P(None, None, 'dp', 'mp')
- qkv_first_new: float32 [2, 3, 768, 768], P(None, None, 'dp', 'mp')
- qkv_second_new: float32 [2, 3, 768, 768], P(None, None, 'dp', 'mp')
- out_weight_new: float32 [2, 768, 768], P(None, 'mp', 'dp')
- out_first_new: float32 [2, 768, 768], P(None, 'mp', 'dp')
- out_second_new: float32 [2, 768, 768], P(None, 'mp', 'dp')
- up_weight_new: float32 [2, 768, 3072], P(None, 'dp', 'mp')
- up_first_new: float32 [2, 768, 3072], P(None, 'dp', 'mp')
- up_second_new: float32 [2, 768, 3072], P(None, 'dp', 'mp')
- down_weight_new: float32 [2, 3072, 768], P(None, 'mp', 'dp')
- down_first_new: float32 [2, 3072, 768], P(None, 'mp', 'dp')
- down_second_new: float32 [2, 3072, 768], P(None, 'mp', 'dp')
- code_table_new: float32 [8192, 768], P('mp', 'dp')
- table_first_new: float32 [8192, 768], P('mp', 'dp')
- table_second_new: float32 [8192, 768], P('mp', 'dp')
- small_params_new: float32 [42144], replicated
- small_first_new: float32 [42144], replicated
- small_second_new: float32 [42144], replicated
- loss_sum: float32 [], replicated
- masked_total: float32 [], replicated
- grad_norm: float32 [], replicated
Inputs may be any that keep to these rules, and one draw needn't show every extreme that they name: `masked_pos`: each row lists 75 different patch numbers of its image. An image's masked patches are the first masked_count entries of its row of masked_pos.
All inputs are finite; a program needn't handle non-finite values.
Results may differ from a plain program's by a relative error of at most 0.0025.
The roundings to bfloat16 on the way count: a program that leaves them out, or rounds other values in their place, can miss the bound.
Values may be sent and summed in bfloat16 or wider, within the bound.
A program may use at most 256 MiB of HBM per device.

v0:
```python
import jax
import jax.numpy as jnp
from jax import lax
from jax.sharding import PartitionSpec as P

D = 768
H = 12
DH = 64
FF = 3072
V = 8192
GRID = 14
LAYERS = 2
MICRO = 2
MAXM = 75
STEP = 10
IMG_MB = 4
SEQ = 197
PATCH = 196
NREL = 732


HIGHEST = lax.Precision.HIGHEST
NORM_EPS = 1e-06
CLIP_NORM = 0.02
LEARN_RATE = 0.03
BETA_ONE = 0.9
BETA_TWO = 0.98
ADAM_EPS = 1e-08
WEIGHT_DECAY = 0.05


def unpack_small(packed):
    first_end = LAYERS * 10 * D
    second_end = first_end + LAYERS * FF
    third_end = second_end + LAYERS * H * NREL
    vectors = packed[:first_end].reshape(LAYERS, 10, D)
    fc_bias = packed[first_end:second_end].reshape(LAYERS, FF)
    rel_tables = packed[second_end:third_end].reshape(LAYERS, H, NREL)
    special = packed[third_end:].reshape(4, D)
    return (vectors, fc_bias, rel_tables, special)


def pack_small(vectors, fc_bias, rel_tables, special):
    return jnp.concatenate(
        [vectors.reshape(-1), fc_bias.reshape(-1), rel_tables.reshape(-1), special.reshape(-1)]
    )


def layer_norm(values, gain_vec, shift_vec):
    average = jnp.mean(values, -1, keepdims=True)
    centred = values - average
    variance = jnp.mean(centred * centred, -1, keepdims=True)
    return centred * lax.rsqrt(variance + NORM_EPS) * gain_vec + shift_vec


def softmax_rows(scores):
    highest = jnp.max(scores, -1, keepdims=True)
    exponent = jnp.exp(scores - highest)
    return exponent / jnp.sum(exponent, -1, keepdims=True)


def exact_gelu(values):
    return jax.nn.gelu(values, approximate=False)


def adam_update(weight, moment_one, moment_two, gradient, factor, decay_rate):
    clipped = gradient * factor
    new_first = BETA_ONE * moment_one + (1.0 - BETA_ONE) * clipped
    new_second = BETA_TWO * moment_two + (1.0 - BETA_TWO) * clipped * clipped
    direction = (
        new_first
        / (1.0 - BETA_ONE**STEP)
        / (jnp.sqrt(new_second / (1.0 - BETA_TWO**STEP)) + ADAM_EPS)
    )
    return (weight - LEARN_RATE * (direction + decay_rate * weight), new_first, new_second)


def gather_rows(values):
    return lax.all_gather(values, "mp", axis=0, tiled=True)


def scatter_rows(values):
    return lax.psum_scatter(values, "mp", scatter_dimension=0, tiled=True)


def place_slice(piece, length, offset):
    return lax.dynamic_update_slice_in_dim(
        jnp.zeros((length,) + piece.shape[1:], jnp.float32), piece, offset, 0
    )


def add_into(running, addend):
    return addend if running is None else jax.tree.map(jnp.add, running, addend)


def stack_of(bundles, position):
    return jnp.stack([bundle[position] for bundle in bundles])


def offset_table():
    extent = 2 * GRID - 1
    place = jnp.arange(GRID)
    return (
        place[:, None, None] - place[None, :, None] + GRID - 1 == jnp.arange(extent)[None, None, :]
    ).astype(jnp.float32)


def bias_block(rel_local, axis_hot):
    heads_here = rel_local.shape[0]
    extent = 2 * GRID - 1
    inner = rel_local[:, : extent * extent].reshape(heads_here, extent, extent)
    across = jnp.einsum("hij,qsj->hiqs", inner, axis_hot, precision=HIGHEST)
    spread = jnp.einsum("hiqs,pri->hpqrs", across, axis_hot, precision=HIGHEST).reshape(
        heads_here, PATCH, PATCH
    )
    top_row = jnp.concatenate(
        [
            rel_local[:, NREL - 1][:, None, None],
            jnp.broadcast_to(rel_local[:, NREL - 3][:, None, None], (heads_here, 1, PATCH)),
        ],
        2,
    )
    lower_rows = jnp.concatenate(
        [jnp.broadcast_to(rel_local[:, NREL - 2][:, None, None], (heads_here, PATCH, 1)), spread], 2
    )
    return jnp.concatenate([top_row, lower_rows], 1)


def bias_grad(score_sums, axis_hot):
    heads_here = score_sums.shape[0]
    extent = 2 * GRID - 1
    inner = score_sums[:, 1:, 1:].reshape(heads_here, GRID, GRID, GRID, GRID)
    across = jnp.einsum("hpqrs,qsj->hprj", inner, axis_hot, precision=HIGHEST)
    folded = jnp.einsum("hprj,pri->hij", across, axis_hot, precision=HIGHEST).reshape(
        heads_here, extent * extent
    )
    extras = jnp.stack(
        [jnp.sum(score_sums[:, 0, 1:], 1), jnp.sum(score_sums[:, 1:, 0], 1), score_sums[:, 0, 0]], 1
    )
    return jnp.concatenate([folded, extras], 1)


def local(
    qkv_weight,
    qkv_first,
    qkv_second,
    out_weight,
    out_first,
    out_second,
    up_weight,
    up_first,
    up_second,
    down_weight,
    down_first,
    down_second,
    code_table,
    table_first,
    table_second,
    small_params,
    small_first,
    small_second,
    patch_codes,
    masked_pos,
    masked_count,
):
    tp_size = lax.axis_size("mp")
    tp_index = lax.axis_index("mp")
    heads_local = H // tp_size
    width_local = D // tp_size
    hidden_local = FF // tp_size
    vocab_local = V // tp_size
    rows_all = IMG_MB * SEQ
    rows_own = rows_all // tp_size
    score_scale = DH ** (-0.5)
    axis_hot = offset_table()
    vectors, fc_bias, rel_tables, special = unpack_small(small_params)
    table_full = lax.all_gather(code_table.astype(jnp.bfloat16), "dp", axis=1, tiled=True)
    count_total = lax.psum(jnp.sum(masked_count).astype(jnp.float32), "dp")
    inverse_total = jnp.ones((), jnp.float32) / count_total

    def own_rows(values):
        return lax.dynamic_slice_in_dim(values, tp_index * rows_own, rows_own, 0)

    def split_heads(values):
        return values.reshape(IMG_MB, SEQ, heads_local, DH)

    def local_slice(vector, length):
        return lax.dynamic_slice_in_dim(vector, tp_index * length, length, 0)

    small_sums = [None] * LAYERS
    matrix_sums = None
    special_sum = None
    loss_sum = jnp.zeros((), jnp.float32)
    for k in range(MICRO):
        first_image = k * IMG_MB
        image_codes = patch_codes[first_image : first_image + IMG_MB]
        masked_spots = masked_pos[first_image : first_image + IMG_MB]
        counts = masked_count[first_image : first_image + IMG_MB]
        valid_slots = jnp.arange(MAXM)[None, :] < counts[:, None]
        hidden_patch = jnp.any(
            (masked_spots[:, :, None] == jnp.arange(PATCH)[None, None, :])
            & valid_slots[:, :, None],
            1,
        )
        batch_masked_rows = jnp.concatenate(
            [jnp.zeros((IMG_MB, 1), jnp.bool_), hidden_patch], 1
        ).reshape(-1)
        batch_cls_rows = jnp.arange(rows_all) % SEQ == 0
        batch_seen_rows = jnp.logical_not(batch_masked_rows | batch_cls_rows)
        row_codes = (
            jnp.concatenate([jnp.zeros((IMG_MB, 1), jnp.int32), image_codes], 1).reshape(-1)
            - tp_index * vocab_local
        )
        inside = batch_seen_rows & (row_codes >= 0) & (row_codes < vocab_local)
        batch_code_hot = (
            inside[:, None] & (row_codes[:, None] == jnp.arange(vocab_local)[None, :])
        ).astype(jnp.bfloat16)
        batch_pick_hot = (masked_spots[:, :, None] + 1 == jnp.arange(SEQ)[None, None, :]).astype(
            jnp.float32
        )
        batch_targets = (
            jnp.take_along_axis(image_codes, masked_spots, 1).reshape(-1) - tp_index * vocab_local
        )
        batch_valid_float = valid_slots.reshape(-1).astype(jnp.float32)
        batch_data = (
            batch_masked_rows,
            batch_cls_rows,
            batch_seen_rows,
            batch_code_hot,
            batch_pick_hot,
            batch_targets,
            batch_valid_float,
            batch_valid_float * inverse_total,
        )
        embed_masked_rows, embed_cls_rows, embed_seen_rows, embed_code_hot = batch_data[:4]
        looked = jnp.dot(embed_code_hot, table_full, preferred_element_type=jnp.float32)
        embedded = scatter_rows(looked)
        fallback = jnp.where(own_rows(embed_cls_rows)[:, None], special[0], special[1])
        x = jnp.where(own_rows(embed_seen_rows)[:, None], embedded, fallback)
        caches = []
        for l in range(LAYERS):
            forward_qkv_local = lax.all_gather(
                qkv_weight[l].astype(jnp.bfloat16), "dp", axis=1, tiled=True
            )
            forward_out_local = lax.all_gather(
                out_weight[l].astype(jnp.bfloat16), "dp", axis=1, tiled=True
            )
            forward_up_local = lax.all_gather(
                up_weight[l].astype(jnp.bfloat16), "dp", axis=0, tiled=True
            )
            forward_down_local = lax.all_gather(
                down_weight[l].astype(jnp.bfloat16), "dp", axis=1, tiled=True
            )
            forward_layer_vec = vectors[l]
            forward_full_attn_in = gather_rows(
                layer_norm(x, forward_layer_vec[0], forward_layer_vec[1]).astype(jnp.bfloat16)
            )
            projected = jnp.einsum(
                "md,cde->cme",
                forward_full_attn_in,
                forward_qkv_local,
                preferred_element_type=jnp.float32,
            )
            forward_query_rows = (
                projected[0] + local_slice(forward_layer_vec[2], width_local)
            ).astype(jnp.bfloat16)
            forward_key_rows = projected[1].astype(jnp.bfloat16)
            forward_value_rows = (
                projected[2] + local_slice(forward_layer_vec[3], width_local)
            ).astype(jnp.bfloat16)
            rel_bias = bias_block(
                lax.dynamic_slice_in_dim(rel_tables[l], tp_index * heads_local, heads_local, 0),
                axis_hot,
            )
            raw_scores = jnp.einsum(
                "bqhd,bkhd->bhqk",
                split_heads(forward_query_rows),
                split_heads(forward_key_rows),
                preferred_element_type=jnp.float32,
            )
            forward_attn_probs = softmax_rows(raw_scores * score_scale + rel_bias[None])
            forward_mixed_heads = (
                jnp.einsum(
                    "bhqk,bkhd->bqhd",
                    forward_attn_probs.astype(jnp.bfloat16),
                    split_heads(forward_value_rows),
                    preferred_element_type=jnp.float32,
                )
                .reshape(rows_all, width_local)
                .astype(jnp.bfloat16)
            )
            forward_attn_out = (
                scatter_rows(
                    jnp.dot(
                        forward_mixed_heads, forward_out_local, preferred_element_type=jnp.float32
                    )
                )
                + forward_layer_vec[4]
            )
            forward_x_mid = x + forward_layer_vec[5] * forward_attn_out
            forward_full_mlp_in = gather_rows(
                layer_norm(forward_x_mid, forward_layer_vec[6], forward_layer_vec[7]).astype(
                    jnp.bfloat16
                )
            )
            forward_pre_act = jnp.dot(
                forward_full_mlp_in, forward_up_local, preferred_element_type=jnp.float32
            ) + local_slice(fc_bias[l], hidden_local)
            forward_activated = exact_gelu(forward_pre_act).astype(jnp.bfloat16)
            forward_mlp_out = (
                scatter_rows(
                    jnp.dot(
                        forward_activated, forward_down_local, preferred_element_type=jnp.float32
                    )
                )
                + forward_layer_vec[8]
            )
            forward_layer_cache = (
                x,
                forward_full_attn_in,
                forward_query_rows,
                forward_key_rows,
                forward_value_rows,
                forward_attn_probs,
                forward_mixed_heads,
                forward_attn_out,
                forward_x_mid,
                forward_full_mlp_in,
                forward_pre_act,
                forward_activated,
                forward_mlp_out,
            )
            x = forward_x_mid + forward_layer_vec[9] * forward_mlp_out
            caches.append(forward_layer_cache)
        pick_hot, targets, valid_float, row_weight = batch_data[4:]
        full_last = gather_rows(layer_norm(x, special[2], special[3]).astype(jnp.bfloat16))
        picked = (
            jnp.einsum(
                "bst,btd->bsd",
                pick_hot.astype(jnp.bfloat16),
                full_last.reshape(IMG_MB, SEQ, D),
                preferred_element_type=jnp.float32,
            )
            .astype(jnp.bfloat16)
            .reshape(IMG_MB * MAXM, D)
        )
        logits = jnp.einsum("nd,vd->nv", picked, table_full, preferred_element_type=jnp.float32)
        target_hits = jnp.arange(vocab_local)[None, :] == targets[:, None]
        target_logit = jnp.sum(jnp.where(target_hits, logits, 0.0), 1)
        local_high = jnp.max(logits, 1)
        highest = lax.pmax(local_high, "mp")
        exp_sums, target_all = lax.psum(
            (jnp.sum(jnp.exp(logits - highest[:, None]), 1), target_logit), "mp"
        )
        log_total = highest + jnp.log(exp_sums)
        loss_part = jnp.sum((log_total - target_all) * valid_float)
        d_logits = (
            (jnp.exp(logits - log_total[:, None]) - target_hits.astype(jnp.float32))
            * row_weight[:, None]
        ).astype(jnp.bfloat16)
        head_d_table = jnp.einsum("nv,nd->vd", d_logits, picked, preferred_element_type=jnp.float32)
        d_picked = jnp.einsum("nv,vd->nd", d_logits, table_full, preferred_element_type=jnp.float32)
        d_full = jnp.einsum(
            "bst,bsd->btd", pick_hot, d_picked.reshape(IMG_MB, MAXM, D), precision=HIGHEST
        ).reshape(rows_all, D)
        d_normed = scatter_rows(d_full)
        unused, pullback = jax.vjp(layer_norm, x, special[2], special[3])
        d_last, d_gain, d_shift = pullback(d_normed)
        loss_part, upstream, d_gain, d_shift, d_head = (
            loss_part,
            d_last,
            d_gain,
            d_shift,
            head_d_table,
        )
        loss_sum = loss_sum + loss_part
        micro_mats = [None] * LAYERS
        for l in reversed(range(LAYERS)):
            backward_layer_cache = caches[l]
            (
                backward_x,
                full_attn_in,
                query_rows,
                key_rows,
                value_rows,
                attn_probs,
                mixed_heads,
                attn_out,
                x_mid,
                full_mlp_in,
                pre_act,
                activated,
                mlp_out,
            ) = backward_layer_cache
            qkv_local = lax.all_gather(qkv_weight[l].astype(jnp.bfloat16), "dp", axis=1, tiled=True)
            out_local = lax.all_gather(out_weight[l].astype(jnp.bfloat16), "dp", axis=1, tiled=True)
            up_local = lax.all_gather(up_weight[l].astype(jnp.bfloat16), "dp", axis=0, tiled=True)
            down_local = lax.all_gather(
                down_weight[l].astype(jnp.bfloat16), "dp", axis=1, tiled=True
            )
            layer_vec = vectors[l]
            g_mlp = (layer_vec[9] * upstream).astype(jnp.bfloat16)
            d_gamma2 = jnp.sum(upstream * mlp_out, 0)
            d_down_bias = jnp.sum(g_mlp.astype(jnp.float32), 0)
            full_g_mlp = gather_rows(g_mlp)
            d_down = jnp.einsum(
                "mf,md->fd", activated, full_g_mlp, preferred_element_type=jnp.float32
            )
            d_act = jnp.einsum(
                "md,fd->mf", full_g_mlp, down_local, preferred_element_type=jnp.float32
            )
            backward_unused, backward_pullback = jax.vjp(exact_gelu, pre_act)
            d_pre = backward_pullback(d_act)[0].astype(jnp.bfloat16)
            d_up_bias = jnp.sum(d_pre.astype(jnp.float32), 0)
            d_up = jnp.einsum("md,mf->df", full_mlp_in, d_pre, preferred_element_type=jnp.float32)
            d_norm2 = scatter_rows(
                jnp.einsum("mf,df->md", d_pre, up_local, preferred_element_type=jnp.float32)
            )
            backward_unused, backward_pullback = jax.vjp(
                layer_norm, x_mid, layer_vec[6], layer_vec[7]
            )
            d_mid, d_gain2, d_shift2 = backward_pullback(d_norm2)
            d_mid = d_mid + upstream
            g_attn = (layer_vec[5] * d_mid).astype(jnp.bfloat16)
            d_gamma1 = jnp.sum(d_mid * attn_out, 0)
            d_out_bias = jnp.sum(g_attn.astype(jnp.float32), 0)
            full_g_attn = gather_rows(g_attn)
            d_out = jnp.einsum(
                "mh,md->hd", mixed_heads, full_g_attn, preferred_element_type=jnp.float32
            )
            d_mixed = split_heads(
                jnp.einsum(
                    "md,hd->mh", full_g_attn, out_local, preferred_element_type=jnp.float32
                ).astype(jnp.bfloat16)
            )
            d_probs = jnp.einsum(
                "bqhd,bkhd->bhqk",
                d_mixed,
                split_heads(value_rows),
                preferred_element_type=jnp.float32,
            )
            d_value = jnp.einsum(
                "bhqk,bqhd->bkhd",
                attn_probs.astype(jnp.bfloat16),
                d_mixed,
                preferred_element_type=jnp.float32,
            ).astype(jnp.bfloat16)
            d_scores = (
                attn_probs * (d_probs - jnp.sum(attn_probs * d_probs, -1, keepdims=True))
            ).astype(jnp.bfloat16)
            d_query = (
                jnp.einsum(
                    "bhqk,bkhd->bqhd",
                    d_scores,
                    split_heads(key_rows),
                    preferred_element_type=jnp.float32,
                )
                * score_scale
            ).astype(jnp.bfloat16)
            d_key = (
                jnp.einsum(
                    "bhqk,bqhd->bkhd",
                    d_scores,
                    split_heads(query_rows),
                    preferred_element_type=jnp.float32,
                )
                * score_scale
            ).astype(jnp.bfloat16)
            score_sums = jnp.sum(d_scores.astype(jnp.float32), 0)
            d_rel = bias_grad(score_sums, axis_hot)
            d_stack = jnp.stack([d_query, d_key, d_value]).reshape(3, rows_all, width_local)
            d_qkv = jnp.einsum(
                "md,cme->cde", full_attn_in, d_stack, preferred_element_type=jnp.float32
            )
            d_norm1 = scatter_rows(
                jnp.einsum("cme,cde->md", d_stack, qkv_local, preferred_element_type=jnp.float32)
            )
            backward_unused, backward_pullback = jax.vjp(
                layer_norm, backward_x, layer_vec[0], layer_vec[1]
            )
            d_input, d_gain1, d_shift1 = backward_pullback(d_norm1)
            column_sums = jnp.sum(d_stack.astype(jnp.float32), 1)
            vec_grad = jnp.stack(
                [
                    d_gain1,
                    d_shift1,
                    place_slice(column_sums[0], D, tp_index * width_local),
                    place_slice(column_sums[2], D, tp_index * width_local),
                    d_out_bias,
                    d_gamma1,
                    d_gain2,
                    d_shift2,
                    d_down_bias,
                    d_gamma2,
                ]
            )
            bundle = (
                d_qkv,
                d_out,
                d_up,
                d_down,
                vec_grad,
                place_slice(d_up_bias, FF, tp_index * hidden_local),
                place_slice(d_rel, H, tp_index * heads_local),
            )
            upstream, bundle = (d_input + d_mid, bundle)
            micro_mats[l] = bundle[:4]
            small_sums[l] = add_into(small_sums[l], bundle[4:])
        masked_rows, cls_rows, seen_rows, code_hot = batch_data[:4]
        d_cls = jnp.sum(jnp.where(own_rows(cls_rows)[:, None], upstream, 0.0), 0)
        d_mask = jnp.sum(jnp.where(own_rows(masked_rows)[:, None], upstream, 0.0), 0)
        seen_grad = jnp.where(own_rows(seen_rows)[:, None], upstream, 0.0).astype(jnp.bfloat16)
        full_seen = gather_rows(seen_grad)
        d_table = jnp.einsum("mv,md->vd", code_hot, full_seen, preferred_element_type=jnp.float32)
        d_cls, d_mask, d_embed = (d_cls, d_mask, d_table)
        special_sum = add_into(special_sum, jnp.stack([d_cls, d_mask, d_gain, d_shift]))
        micro_grads = (
            stack_of(micro_mats, 0),
            stack_of(micro_mats, 1),
            stack_of(micro_mats, 2),
            stack_of(micro_mats, 3),
            d_head + d_embed,
        )
        matrix_sums = add_into(matrix_sums, micro_grads)
    matrix_sums = (
        lax.psum_scatter(matrix_sums[0], "dp", scatter_dimension=2, tiled=True),
        lax.psum_scatter(matrix_sums[1], "dp", scatter_dimension=2, tiled=True),
        lax.psum_scatter(matrix_sums[2], "dp", scatter_dimension=1, tiled=True),
        lax.psum_scatter(matrix_sums[3], "dp", scatter_dimension=2, tiled=True),
        lax.psum_scatter(matrix_sums[4], "dp", scatter_dimension=1, tiled=True),
    )
    grad_qkv, grad_out, grad_up, grad_down, grad_table = matrix_sums
    grad_small = lax.psum(
        pack_small(
            stack_of(small_sums, 0), stack_of(small_sums, 1), stack_of(small_sums, 2), special_sum
        ),
        ("dp", "mp"),
    )
    own_squares = sum(
        (jnp.sum(g * g) for g in (grad_qkv, grad_out, grad_up, grad_down, grad_table))
    )
    first_member = jnp.where(tp_index == 0, 1.0, 0.0)
    squares_all, loss_total = lax.psum((own_squares, loss_sum * first_member), ("dp", "mp"))
    grad_norm = jnp.sqrt(squares_all + jnp.sum(grad_small * grad_small))
    factor = jnp.minimum(1.0, CLIP_NORM / (grad_norm + 1e-06))
    qkv_new, qkv_one, qkv_two = adam_update(
        qkv_weight, qkv_first, qkv_second, grad_qkv, factor, WEIGHT_DECAY
    )
    out_new, out_one, out_two = adam_update(
        out_weight, out_first, out_second, grad_out, factor, WEIGHT_DECAY
    )
    up_new, up_one, up_two = adam_update(
        up_weight, up_first, up_second, grad_up, factor, WEIGHT_DECAY
    )
    down_new, down_one, down_two = adam_update(
        down_weight, down_first, down_second, grad_down, factor, WEIGHT_DECAY
    )
    table_new, table_one, table_two = adam_update(
        code_table, table_first, table_second, grad_table, factor, WEIGHT_DECAY
    )
    small_new, small_one, small_two = adam_update(
        small_params, small_first, small_second, grad_small, factor, 0.0
    )
    return (
        qkv_new,
        qkv_one,
        qkv_two,
        out_new,
        out_one,
        out_two,
        up_new,
        up_one,
        up_two,
        down_new,
        down_one,
        down_two,
        table_new,
        table_one,
        table_two,
        small_new,
        small_one,
        small_two,
        loss_total,
        count_total,
        grad_norm,
    )


def solution(mesh):
    in_specs = (
        P(None, None, "dp", "mp"),
        P(None, None, "dp", "mp"),
        P(None, None, "dp", "mp"),
        P(None, "mp", "dp"),
        P(None, "mp", "dp"),
        P(None, "mp", "dp"),
        P(None, "dp", "mp"),
        P(None, "dp", "mp"),
        P(None, "dp", "mp"),
        P(None, "mp", "dp"),
        P(None, "mp", "dp"),
        P(None, "mp", "dp"),
        P("mp", "dp"),
        P("mp", "dp"),
        P("mp", "dp"),
        P(),
        P(),
        P(),
        P("dp", None),
        P("dp", None),
        P("dp"),
    )
    out_specs = (
        P(None, None, "dp", "mp"),
        P(None, None, "dp", "mp"),
        P(None, None, "dp", "mp"),
        P(None, "mp", "dp"),
        P(None, "mp", "dp"),
        P(None, "mp", "dp"),
        P(None, "dp", "mp"),
        P(None, "dp", "mp"),
        P(None, "dp", "mp"),
        P(None, "mp", "dp"),
        P(None, "mp", "dp"),
        P(None, "mp", "dp"),
        P("mp", "dp"),
        P("mp", "dp"),
        P("mp", "dp"),
        P(),
        P(),
        P(),
        P(),
        P(),
        P(),
    )
    return jax.shard_map(local, mesh=mesh, in_specs=in_specs, out_specs=out_specs, check_vma=False)
```

profile of v0, /device:TPU:0, one launch (start us, length us, event | category | flops | bytes accessed | tf_op | source)
XLA Modules:
  0.0 2516.3 jit_solution(6102536425156746271)
XLA Ops:
  23.8 21.7 all-gather.54.cloned.1.call-done
  56.9 87.0 %fusion.329 = (f32[200,768]{1,0:T(8,128)S(1)}, f32[200,768]{1,0:T(8,128)S(1)}) fusion(f32[788,768]{1,0:T(8,128)} %fusion.32, f32[788,768]{1,0:T(8,128)} %fusion.27), kind=kCustom, calls=%all-reduce-scatter.29 | all-reduce-scatter fusion | flops 1228801 | bytes 6070784
  157.7 12.0 all-gather
  183.3 10.9 all-gather.1
  200.7 17.2 all-gather.64.cloned.1.call-done
  252.1 85.9 %fusion.328 = (f32[200,768]{1,0:T(8,128)S(1)}, f32[200,768]{1,0:T(8,128)S(1)}) fusion(f32[788,768]{1,0:T(8,128)} %fusion.218, f32[788,768]{1,0:T(8,128)} %fusion.215), kind=kCustom, calls=%all-reduce-scatter.28 | all-reduce-scatter fusion | flops 1228801 | bytes 6070784
  355.7 27.7 %all-gather.66.cloned.1.call-done = bf16[4,197,768]{2,1,0:T(8,128)(2,1)} async-done(((bf16[1,197,768]{2,1,0:T(8,128)(2,1)}), bf16[4,197,768]{2,1,0:T(8,128)(2,1)}) %all-gather.66.cloned.1.call-update) | async-done | bytes 1210384 | tf_op jit(solution)/shard_map/all_gather | solution.py:79
  385.1 30.8 %all-gather.84.cloned.1.call-done = bf16[4,197,768]{2,1,0:T(8,128)(2,1)} async-done(((bf16[1,197,768]{2,1,0:T(8,128)(2,1)}), bf16[4,197,768]{2,1,0:T(8,128)(2,1)}) %all-gather.84.cloned.1.call-update) | async-done | bytes 1210384 | tf_op jit(solution)/shard_map/all_gather | solution.py:79
  418.6 22.7 all-gather.56.cloned.1.call-done
  445.3 13.5 multiply_convert_fusion.7
  458.8 9.0 all-gather.58.cloned.1.call-done
  474.8 86.9 %fusion.327 = (f32[200,768]{1,0:T(8,128)S(1)}, f32[200,768]{1,0:T(8,128)S(1)}) fusion(f32[788,768]{1,0:T(8,128)} %fusion.128, f32[788,768]{1,0:T(8,128)} %fusion.124), kind=kCustom, calls=%all-reduce-scatter.27 | all-reduce-scatter fusion | flops 1228801 | bytes 6070784
  576.2 12.0 all-gather.4
  604.2 10.9 all-gather.5
  621.5 17.5 all-gather.68.cloned.1.call-done
  670.1 85.9 %fusion.326 = (f32[200,768]{1,0:T(8,128)S(1)}, f32[200,768]{1,0:T(8,128)S(1)}) fusion(f32[788,768]{1,0:T(8,128)} %fusion.212, f32[788,768]{1,0:T(8,128)} %fusion.209), kind=kCustom, calls=%all-reduce-scatter.26 | all-reduce-scatter fusion | flops 1228801 | bytes 6070784
  773.5 27.9 %all-gather.70.cloned.1.call-done = bf16[4,197,768]{2,1,0:T(8,128)(2,1)} async-done(((bf16[1,197,768]{2,1,0:T(8,128)(2,1)}), bf16[4,197,768]{2,1,0:T(8,128)(2,1)}) %all-gather.70.cloned.1.call-update) | async-done | bytes 1210384 | tf_op jit(solution)/shard_map/all_gather | solution.py:79
  804.0 29.9 %all-gather.88.cloned.1.call-done = bf16[4,197,768]{2,1,0:T(8,128)(2,1)} async-done(((bf16[1,197,768]{2,1,0:T(8,128)(2,1)}), bf16[4,197,768]{2,1,0:T(8,128)(2,1)}) %all-gather.88.cloned.1.call-update) | async-done | bytes 1210384 | tf_op jit(solution)/shard_map/all_gather | solution.py:79
  836.6 22.8 all-gather.60.cloned.1.call-done
  863.8 13.5 multiply_convert_fusion.6
  877.3 8.6 all-gather.62.cloned.1.call-done
  893.0 86.9 %fusion.325 = (f32[200,768]{1,0:T(8,128)S(1)}, f32[200,768]{1,0:T(8,128)S(1)}) fusion(f32[788,768]{1,0:T(8,128)} %fusion.108, f32[788,768]{1,0:T(8,128)} %fusion.104), kind=kCustom, calls=%all-reduce-scatter.25 | all-reduce-scatter fusion | flops 1228801 | bytes 6070784
  997.4 12.5 psum.57
  1011.0 15.0 all-gather.90.cloned.1.call-done
  1027.8 30.0 %all-gather.72.cloned.1.call-done = bf16[4,197,768]{2,1,0:T(8,128)(2,1)} async-done(((bf16[1,197,768]{2,1,0:T(8,128)(2,1)}), bf16[4,197,768]{2,1,0:T(8,128)(2,1)}) %all-gather.72.cloned.1.call-update) | async-done | bytes 1210384 | tf_op jit(solution)/shard_map/all_gather | solution.py:79
  1066.3 10.1 all-reduce.47
  1079.9 9.0 all-reduce.46
  1115.7 82.8 %fusion.324 = (f32[200,768]{1,0:T(8,128)S(1)}, f32[200,768]{1,0:T(8,128)S(1)}) fusion(f32[788,768]{1,0:T(8,128)} %reshape.1568, f32[788,768]{1,0:T(8,128)} %reshape.1575), kind=kCustom, calls=%all-reduce-scatter.24 | all-reduce-scatter fusion | flops 1228801 | bytes 6070784
  1213.1 31.6 %all-gather.92.cloned.1.call-done = bf16[4,197,768]{2,1,0:T(8,128)(2,1)} async-done(((bf16[1,197,768]{2,1,0:T(8,128)(2,1)}), bf16[4,197,768]{2,1,0:T(8,128)(2,1)}) %all-gather.92.cloned.1.call-update) | async-done | bytes 1210384 | tf_op jit(solution)/shard_map/all_gather | solution.py:79
  1255.6 20.9 all-gather.74.cloned.1.call-done
  1287.4 86.7 %fusion.323 = (f32[200,768]{1,0:T(8,128)}, f32[200,768]{1,0:T(8,128)}) fusion(f32[788,768]{1,0:T(8,128)} %fusion.118, f32[788,768]{1,0:T(8,128)} %fusion.114), kind=kCustom, calls=%all-reduce-scatter.23 | all-reduce-scatter fusion | flops 1228801 | bytes 6070784
  1396.9 28.9 %all-gather.94.cloned.1.call-done = bf16[4,197,768]{2,1,0:T(8,128)(2,1)} async-done(((bf16[1,197,768]{2,1,0:T(8,128)(2,1)}), bf16[4,197,768]{2,1,0:T(8,128)(2,1)}) %all-gather.94.cloned.1.call-update) | async-done | bytes 1210384 | tf_op jit(solution)/shard_map/all_gather | solution.py:79
  1438.1 19.7 all-gather.76.cloned.1.call-done
  1483.8 85.9 %fusion.322 = (f32[200,768]{1,0:T(8,128)S(1)}, f32[200,768]{1,0:T(8,128)S(1)}) fusion(f32[788,768]{1,0:T(8,128)} %convolution_bitcast_fusion.5, f32[788,768]{1,0:T(8,128)} %convolution_bitcast_fusion.4), kind=kCustom, calls=%all-reduce-scatter.22 | all-reduce-scatter fusion | flops 1228801 | bytes 6070784
  1583.6 30.5 %all-gather.96.cloned.1.call-done = bf16[4,197,768]{2,1,0:T(8,128)(2,1)} async-done(((bf16[1,197,768]{2,1,0:T(8,128)(2,1)}), bf16[4,197,768]{2,1,0:T(8,128)(2,1)}) %all-gather.96.cloned.1.call-update) | async-done | bytes 1210384 | tf_op jit(solution)/shard_map/all_gather | solution.py:79
  1625.0 21.7 all-gather.78.cloned.1.call-done
  1657.6 85.9 %fusion.321 = (f32[200,768]{1,0:T(8,128)S(1)}, f32[200,768]{1,0:T(8,128)S(1)}) fusion(f32[788,768]{1,0:T(8,128)} %fusion.138, f32[788,768]{1,0:T(8,128)} %fusion.134), kind=kCustom, calls=%all-reduce-scatter.21 | all-reduce-scatter fusion | flops 1228801 | bytes 6070784
  1758.3 30.1 %all-gather.98.cloned.1.call-done = bf16[4,197,768]{2,1,0:T(8,128)(2,1)} async-done(((bf16[1,197,768]{2,1,0:T(8,128)(2,1)}), bf16[4,197,768]{2,1,0:T(8,128)(2,1)}) %all-gather.98.cloned.1.call-update) | async-done | bytes 1210384 | tf_op jit(solution)/shard_map/all_gather | solution.py:79
  1799.8 21.1 all-gather.80.cloned.1.call-done
  1848.4 86.6 %fusion.320 = (f32[200,768]{1,0:T(8,128)}, f32[200,768]{1,0:T(8,128)S(1)}) fusion(f32[788,768]{1,0:T(8,128)} %convolution_bitcast_fusion.2, f32[788,768]{1,0:T(8,128)} %convolution_bitcast_fusion.3), kind=kCustom, calls=%all-reduce-scatter.20 | all-reduce-scatter fusion | flops 1228801 | bytes 6070784
  1964.1 8.2 copy.770
  2007.9 8.0 reshape.1712
  2107.6 37.3 %reduce-scatter.55.cloned.1.call-done = f32[96,384]{1,0:T(8,128)} async-done(((f32[768,384]{1,0:T(8,128)}), f32[96,384]{1,0:T(8,128)}) %reduce-scatter.55.cloned.1.call-update) | async-done | bytes 147472
  2146.7 55.5 %reduce-scatter.49.cloned.1.call-done = f32[2,96,768]{2,1,0:T(8,128)} async-done(((f32[2,768,768]{2,1,0:T(8,128)}), f32[2,96,768]{2,1,0:T(8,128)}) %reduce-scatter.49.cloned.1.call-update) | async-done | bytes 589840 | tf_op jit(solution)/shard_map/reduce_scatter | solution.py:528
  2204.0 50.1 %reduce-scatter.53.cloned.1.call-done = f32[96,1152]{1,0:T(8,128)} async-done(((f32[768,1152]{1,0:T(8,128)}), f32[96,1152]{1,0:T(8,128)}) %reduce-scatter.53.cloned.1.call-update) | async-done | bytes 442384
  2259.4 60.2 %reduce-scatter.51.cloned.1.call-done = f32[2048,96]{0,1:T(8,128)} async-done(((f32[2048,768]{0,1:T(8,128)}), f32[2048,96]{0,1:T(8,128)}) %reduce-scatter.51.cloned.1.call-update) | async-done | bytes 786448 | tf_op jit(solution)/shard_map/reduce_scatter | solution.py:530
  2322.2 125.4 %all-reduce.61.cloned.1.call-done = f32[42144]{0:T(1024)} async-done(((f32[42144]{0:T(1024)}), f32[42144]{0:T(1024)}) %all-reduce.61.cloned.1.call-update) | async-done | bytes 168592 | tf_op jit(solution)/shard_map/psum | solution.py:533
  2449.1 42.2 %all-reduce.45 = (f32[]{:T(128)}, f32[]{:T(128)}) all-reduce(f32[]{:T(128)S(6)} %add.858, f32[]{:T(128)S(6)} %mul.1570), channel_id=1, replica_groups=mesh['dp'=8,'mp'=4] {'dp','mp'}, use_global_device_ids=true, to_apply=%region_94.96 | all-reduce | flops 2 | bytes 16 | tf_op jit(solution)/shard_map/psum | solution.py:543
  (1453 shorter events, 648.7 us)
Async XLA Ops:
  7.2 38.3 %all-gather.54.cloned.1.call-start = ((), (), s32[]{:S(2)}) async-start(), calls=%async_computation.4 | async-start | bytes 3538944 | tf_op jit(solution)/shard_map/all_gather | solution.py:177
  9.2 185.6 %all-gather.82.cloned.1.call-start = ((), (), s32[]{:S(2)}) async-start(), calls=%async_computation.21 | async-start | bytes 1536000 | tf_op jit(solution)/shard_map/all_gather | solution.py:79
  144.0 6.8 collective-permute-start
  147.4 3.9 collective-permute-start.9
  154.6 63.2 %all-gather.64.cloned.1.call-start = ((), (), s32[]{:S(2)}) async-start(), calls=%async_computation.12 | async-start | bytes 1536000 | tf_op jit(solution)/shard_map/all_gather | solution.py:79
  157.6 225.8 %all-gather.66.cloned.1.call-start = ((), (), s32[]{:S(2)}) async-start(), calls=%async_computation.13 | async-start | bytes 1536000 | tf_op jit(solution)/shard_map/all_gather | solution.py:79
  338.1 5.0 collective-permute-start.1
  341.0 4.2 collective-permute-start.10
  352.7 63.2 %all-gather.84.cloned.1.call-start = ((), (), s32[]{:S(2)}) async-start(), calls=%async_computation.22 | async-start | bytes 1536000 | tf_op jit(solution)/shard_map/all_gather | solution.py:79
  353.3 88.0 %all-gather.56.cloned.1.call-start = ((), (), s32[]{:S(2)}) async-start(), calls=%async_computation.8 | async-start | bytes 1327104 | tf_op jit(solution)/shard_map/all_gather | solution.py:248
  354.1 113.7 %all-gather.58.cloned.1.call-start = ((), (), s32[]{:S(2)}) async-start(), calls=%async_computation.9 | async-start | bytes 1327104 | tf_op jit(solution)/shard_map/all_gather | solution.py:251
  355.0 261.8 %all-gather.86.cloned.1.call-start = ((), (), s32[]{:S(2)}) async-start(), calls=%async_computation.23 | async-start | bytes 1536000 | tf_op jit(solution)/shard_map/all_gather | solution.py:79
  561.8 5.3 collective-permute-start.2
  565.2 3.7 collective-permute-start.11
  575.4 63.6 %all-gather.68.cloned.1.call-start = ((), (), s32[]{:S(2)}) async-start(), calls=%async_computation.14 | async-start | bytes 1536000 | tf_op jit(solution)/shard_map/all_gather | solution.py:79
  576.1 225.2 %all-gather.70.cloned.1.call-start = ((), (), s32[]{:S(2)}) async-start(), calls=%async_computation.15 | async-start | bytes 1536000 | tf_op jit(solution)/shard_map/all_gather | solution.py:79
  756.1 5.0 collective-permute-start.3
  759.0 4.2 collective-permute-start.12
  770.6 63.3 %all-gather.88.cloned.1.call-start = ((), (), s32[]{:S(2)}) async-start(), calls=%async_computation.24 | async-start | bytes 1536000 | tf_op jit(solution)/shard_map/all_gather | solution.py:79
  771.3 88.0 %all-gather.60.cloned.1.call-start = ((), (), s32[]{:S(2)}) async-start(), calls=%async_computation.10 | async-start | bytes 1327104 | tf_op jit(solution)/shard_map/all_gather | solution.py:248
  771.9 114.0 %all-gather.62.cloned.1.call-start = ((), (), s32[]{:S(2)}) async-start(), calls=%async_computation.11 | async-start | bytes 1327104 | tf_op jit(solution)/shard_map/all_gather | solution.py:251
  772.6 253.3 %all-gather.90.cloned.1.call-start = ((), (), s32[]{:S(2)}) async-start(), calls=%async_computation.25 | async-start | bytes 1536000 | tf_op jit(solution)/shard_map/all_gather | solution.py:79
  979.9 5.3 collective-permute-start.4
  984.0 4.2 collective-permute-start.13
  995.4 62.3 %all-gather.72.cloned.1.call-start = ((), (), s32[]{:S(2)}) async-start(), calls=%async_computation.16 | async-start | bytes 1536000 | tf_op jit(solution)/shard_map/all_gather | solution.py:79
  996.0 248.7 %all-gather.92.cloned.1.call-start = ((), (), s32[]{:S(2)}) async-start(), calls=%async_computation.26 | async-start | bytes 1536000 | tf_op jit(solution)/shard_map/all_gather | solution.py:79
  1212.1 64.5 %all-gather.74.cloned.1.call-start = ((), (), s32[]{:S(2)}) async-start(), calls=%async_computation.17 | async-start | bytes 1536000 | tf_op jit(solution)/shard_map/all_gather | solution.py:79
  1212.7 213.2 %all-gather.94.cloned.1.call-start = ((), (), s32[]{:S(2)}) async-start(), calls=%async_computation.27 | async-start | bytes 1536000 | tf_op jit(solution)/shard_map/all_gather | solution.py:79
  1375.0 5.6 collective-permute-start.15
  1379.3 5.6 collective-permute-start.6
  1395.9 61.9 %all-gather.76.cloned.1.call-start = ((), (), s32[]{:S(2)}) async-start(), calls=%async_computation.18 | async-start | bytes 1536000 | tf_op jit(solution)/shard_map/all_gather | solution.py:79
  1396.7 217.4 %all-gather.96.cloned.1.call-start = ((), (), s32[]{:S(2)}) async-start(), calls=%async_computation.28 | async-start | bytes 1536000 | tf_op jit(solution)/shard_map/all_gather | solution.py:79
  1569.8 5.0 collective-permute-start.16
  1572.8 3.7 collective-permute-start.7
  1582.8 63.9 %all-gather.78.cloned.1.call-start = ((), (), s32[]{:S(2)}) async-start(), calls=%async_computation.19 | async-start | bytes 1536000 | tf_op jit(solution)/shard_map/all_gather | solution.py:79
  1583.6 204.9 %all-gather.98.cloned.1.call-start = ((), (), s32[]{:S(2)}) async-start(), calls=%async_computation.29 | async-start | bytes 1536000 | tf_op jit(solution)/shard_map/all_gather | solution.py:79
  1743.6 5.0 collective-permute-start.17
  1757.1 63.9 %all-gather.80.cloned.1.call-start = ((), (), s32[]{:S(2)}) async-start(), calls=%async_computation.20 | async-start | bytes 1536000 | tf_op jit(solution)/shard_map/all_gather | solution.py:79
  1757.9 264.6 %all-gather.100.cloned.1.call-start = ((), (), s32[]{:S(2)}) async-start(), calls=%async_computation.30 | async-start | bytes 1536000 | tf_op jit(solution)/shard_map/all_gather | solution.py:79
  1936.2 5.0 collective-permute-start.19
  1939.1 4.2 collective-permute-start.18
  1952.1 72.3 %all-gather.102.cloned.1.call-start = ((), (), s32[]{:S(2)}) async-start(), calls=%async_computation.31 | async-start | bytes 1536000 | tf_op jit(solution)/shard_map/all_gather | solution.py:79
  1953.0 151.5 %all-reduce.63.cloned.1.call-start = ((), (), s32[]{:S(2)}) async-start(), calls=%async_computation.34 | async-start | bytes 9437184
  1972.3 172.5 %reduce-scatter.55.cloned.1.call-start = ((), (), s32[]{:S(2)}) async-start(), calls=%async_computation.33 | async-start | bytes 1327104
  1979.4 222.9 %reduce-scatter.49.cloned.1.call-start = ((), (), s32[]{:S(2)}) async-start(), calls=%async_computation.5 | async-start | bytes 5308416 | tf_op jit(solution)/shard_map/reduce_scatter | solution.py:528
  1989.8 264.3 %reduce-scatter.53.cloned.1.call-start = ((), (), s32[]{:S(2)}) async-start(), calls=%async_computation.32 | async-start | bytes 3981312
  2015.9 303.7 %reduce-scatter.51.cloned.1.call-start = ((), (), s32[]{:S(2)}) async-start(), calls=%async_computation.6 | async-start | bytes 7077888 | tf_op jit(solution)/shard_map/reduce_scatter | solution.py:530
  2039.9 407.7 %all-reduce.61.cloned.1.call-start = ((), (), s32[]{:S(2)}) async-start(), calls=%async_computation.7 | async-start | bytes 344064 | tf_op jit(solution)/shard_map/psum | solution.py:533
  (388 other events, 8451.8 us)
Sparse Core Ops, SparseCore 0:
  10.5 35.0 all-gather.53
  154.8 30.5 all-gather.81
  187.5 30.3 all-gather.63
  352.8 30.6 all-gather.65
  385.4 30.3 all-gather.83
  418.1 23.1 all-gather.55
  443.7 24.0 all-gather.57
  575.5 30.8 all-gather.85
  608.6 30.3 all-gather.67
  770.7 30.5 all-gather.69
  803.5 30.3 all-gather.87
  836.2 23.1 all-gather.59
  861.8 24.0 all-gather.61
  995.6 30.3 all-gather.89
  1027.3 30.3 all-gather.71
  1212.2 32.4 all-gather.91
  1246.2 30.3 all-gather.73
  1396.0 29.7 all-gather.93
  1427.4 30.3 all-gather.75
  1582.9 31.1 all-gather.95
  1616.3 30.3 all-gather.77
  1757.2 31.1 all-gather.97
  1790.6 30.3 all-gather.79
  1952.2 30.6 all-gather.99
  1985.0 30.3 all-gather.101
  2018.6 85.9 all-reduce.62
  2108.0 36.8 reduce-scatter.54
  2148.3 53.8 reduce-scatter.48
  2206.1 48.0 reduce-scatter.52
  2257.8 61.7 reduce-scatter.50
  2325.7 121.7 all-reduce.60
where the time goes:
time: 2530 us; the launch traced here: 2520 us
  blocking collectives  980 us (39%)
  waiting for transfers between devices  831 us (33%)
  local copies, waits for them, and re-layouts  273 us (11%)
  matrix products  262 us (10%)
  other arithmetic  87.7 us (3%)
  starting transfers between devices  51.7 us (2%)
  between operations  30.5 us (1%)
    unnamed x10, blocking collectives  860 us
    all_gather x20, waiting for transfers between devices, gather_rows(): return lax.all_gather(values, 'mp', axis=0, tiled=True)  400 us
    unnamed x863, local copies, waits for them, and re-layouts  140 us
    psum x1, waiting for transfers between devices, local(): lax.psum(pack_small(stack_of(small_sums, 0), stack_of(small_sums, 1), sta...  125 us
    unnamed x54, waiting for transfers between devices  105 us
    reduce_scatter x1, waiting for transfers between devices, local(): lax.psum_scatter(matrix_sums[4], 'dp', scatter_dimension=1, tiled=True)  60.2 us
    reduce_scatter x1, waiting for transfers between devices, local(): lax.psum_scatter(matrix_sums[2], 'dp', scatter_dimension=1, tiled=True)  55.5 us
  transfers between devices with their start and end apart: 51, of which 31 were waited for; matrix products, arithmetic and copies ran while one was open for 12% of the time, Pallas kernels for 0%

commit v1 on v0

v1 whole, which is shorter than its diff:
```python
import functools

import jax
import jax.numpy as jnp
from jax import lax
from jax.experimental import pallas as pl
from jax.experimental.pallas import tpu as pltpu
from jax.sharding import PartitionSpec as P

D = 768
H = 12
DH = 64
FF = 3072
V = 8192
GRID = 14
LAYERS = 2
MAXM = 75
STEP = 10
SEQ = 197
PATCH = 196
NREL = 732


MESH = pl.DeviceIdType.MESH
HIGHEST = lax.Precision.HIGHEST
NORM_EPS = 1e-06
CLIP_NORM = 0.02
LEARN_RATE = 0.03
BETA_ONE = 0.9
BETA_TWO = 0.98
ADAM_EPS = 1e-08
WEIGHT_DECAY = 0.05


def unpack_small(packed):
    first_end = LAYERS * 10 * D
    second_end = first_end + LAYERS * FF
    third_end = second_end + LAYERS * H * NREL
    vectors = packed[:first_end].reshape(LAYERS, 10, D)
    fc_bias = packed[first_end:second_end].reshape(LAYERS, FF)
    rel_tables = packed[second_end:third_end].reshape(LAYERS, H, NREL)
    special = packed[third_end:].reshape(4, D)
    return (vectors, fc_bias, rel_tables, special)


def pack_small(vectors, fc_bias, rel_tables, special):
    return jnp.concatenate(
        [vectors.reshape(-1), fc_bias.reshape(-1), rel_tables.reshape(-1), special.reshape(-1)]
    )


def layer_norm(values, gain_vec, shift_vec):
    average = jnp.mean(values, -1, keepdims=True)
    centred = values - average
    variance = jnp.mean(centred * centred, -1, keepdims=True)
    return centred * lax.rsqrt(variance + NORM_EPS) * gain_vec + shift_vec


def softmax_rows(scores):
    highest = jnp.max(scores, -1, keepdims=True)
    exponent = jnp.exp(scores - highest)
    return exponent / jnp.sum(exponent, -1, keepdims=True)


def exact_gelu(values):
    return jax.nn.gelu(values, approximate=False)


def adam_update(weight, moment_one, moment_two, gradient, factor, decay_rate):
    clipped = gradient * factor
    new_first = BETA_ONE * moment_one + (1.0 - BETA_ONE) * clipped
    new_second = BETA_TWO * moment_two + (1.0 - BETA_TWO) * clipped * clipped
    direction = (
        new_first
        / (1.0 - BETA_ONE**STEP)
        / (jnp.sqrt(new_second / (1.0 - BETA_TWO**STEP)) + ADAM_EPS)
    )
    return (weight - LEARN_RATE * (direction + decay_rate * weight), new_first, new_second)


def offset_table():
    extent = 2 * GRID - 1
    place = jnp.arange(GRID)
    return (
        place[:, None, None] - place[None, :, None] + GRID - 1 == jnp.arange(extent)[None, None, :]
    ).astype(jnp.float32)


def bias_block(rel_local, axis_hot):
    heads_here = rel_local.shape[0]
    extent = 2 * GRID - 1
    inner = rel_local[:, : extent * extent].reshape(heads_here, extent, extent)
    across = jnp.einsum("hij,qsj->hiqs", inner, axis_hot, precision=HIGHEST)
    spread = jnp.einsum("hiqs,pri->hpqrs", across, axis_hot, precision=HIGHEST).reshape(
        heads_here, PATCH, PATCH
    )
    top_row = jnp.concatenate(
        [
            rel_local[:, NREL - 1][:, None, None],
            jnp.broadcast_to(rel_local[:, NREL - 3][:, None, None], (heads_here, 1, PATCH)),
        ],
        2,
    )
    lower_rows = jnp.concatenate(
        [jnp.broadcast_to(rel_local[:, NREL - 2][:, None, None], (heads_here, PATCH, 1)), spread], 2
    )
    return jnp.concatenate([top_row, lower_rows], 1)


def bias_grad(score_sums, axis_hot):
    heads_here = score_sums.shape[0]
    extent = 2 * GRID - 1
    inner = score_sums[:, 1:, 1:].reshape(heads_here, GRID, GRID, GRID, GRID)
    across = jnp.einsum("hpqrs,qsj->hprj", inner, axis_hot, precision=HIGHEST)
    folded = jnp.einsum("hprj,pri->hij", across, axis_hot, precision=HIGHEST).reshape(
        heads_here, extent * extent
    )
    extras = jnp.stack(
        [jnp.sum(score_sums[:, 0, 1:], 1), jnp.sum(score_sums[:, 1:, 0], 1), score_sums[:, 0, 0]], 1
    )
    return jnp.concatenate([folded, extras], 1)


def factor(ndp):
    half = ndp // 2
    inner = 1
    while inner * inner < half:
        inner *= 2
    return half // inner, inner


class Place:
    def __init__(self, outer, inner, members):
        index = lax.axis_index("dp")
        self.sizes = {"a": outer, "b": inner, "c": 2, "m": members}
        self.at = {
            "a": lax.div(index, 2 * inner),
            "b": lax.rem(lax.div(index, 2), inner),
            "c": lax.rem(index, 2),
            "m": lax.axis_index("mp"),
        }

    def shifted(self, axis, step):
        size = self.sizes[axis]
        return lax.rem(self.at[axis] + (step + size) % size, size)

    def device(self, axis, step):
        spot = dict(self.at)
        spot[axis] = self.shifted(axis, step)
        return ((spot["a"] * self.sizes["b"] + spot["b"]) * 2 + spot["c"], spot["m"])

    def enter(self):
        barrier = pltpu.get_barrier_semaphore()
        total = 0
        for axis, size in self.sizes.items():
            for step in range(1, size):
                pl.semaphore_signal(
                    barrier, inc=1, device_id=self.device(axis, step), device_id_type=MESH
                )
                total += 1
        pl.semaphore_wait(barrier, total)


def gather_kernel(outer, inner, members, groups, count, look, *refs):
    ins = refs[:count]
    outs = refs[count : 2 * count]
    send, recv, own = refs[2 * count :]
    place = Place(outer, inner, members)
    a, b, c, m = (place.at[axis] for axis in "abcm")
    place.enter()
    used = [0]

    def copies(piece, stage):
        i, first_row, rows, order = piece
        out = outs[i]
        width = ins[i].shape[1]
        span = pl.ds(first_row, rows)
        if stage == 0:
            axis, src = "m", ins[i].at[span]
            dst = out.at[a, b, c, span, pl.ds(pl.multiple_of(m * width, 128), width)]
        elif stage == 3:
            axis, src = "c", out.at[:, :, c, span]
            dst = src
        else:
            axis = order[stage - 1]
            if stage == 1:
                src = out.at[a, b, c, span]
            elif axis == "a":
                src = out.at[a, :, c, span]
            else:
                src = out.at[:, b, c, span]
            dst = src
        made = []
        for step in range(1, place.sizes[axis]):
            k = used[0]
            used[0] += 1
            made.append(
                pltpu.make_async_remote_copy(
                    src_ref=src,
                    dst_ref=dst,
                    send_sem=send.at[k],
                    recv_sem=recv.at[k],
                    device_id=place.device(axis, step),
                    device_id_type=MESH,
                )
            )
        return made

    flying = {}

    def start(group, stage):
        made = [copy for piece in groups[group] for copy in copies(piece, stage)]
        for copy in made:
            copy.start()
        flying[group, stage] = made

    total = len(groups)
    for group in range(min(look, total)):
        start(group, 0)
    local = []
    for i in range(count):
        width = ins[i].shape[1]
        mine = pl.ds(pl.multiple_of(m * width, 128), width)
        local.append(pltpu.make_async_copy(ins[i], outs[i].at[a, b, c, :, mine], own.at[i]))
    for copy in local:
        copy.start()
    for copy in local:
        copy.wait()
    for tick in range(total + 3):
        if tick + look < total:
            start(tick + look, 0)
        for stage in (2, 1, 0, 3):
            group = tick - stage
            if 0 <= group < total:
                for copy in flying[group, stage]:
                    copy.wait_recv()
                if stage < 3:
                    start(group, stage + 1)
    for made in flying.values():
        for copy in made:
            copy.wait_send()


def gather_blocks(blocks, ndp, members):
    outer, inner = factor(ndp)
    groups = []
    for i, block in enumerate(blocks):
        rows = block.shape[0]
        if rows % 32:
            groups.append([(i, 0, rows, "ab")])
        else:
            groups.append([(i, 0, rows // 2, "ab"), (i, rows // 2, rows // 2, "ba")])
    count = len(blocks)
    peers = (outer - 1) + (inner - 1) + 1 + (members - 1)
    sems = sum(len(group) for group in groups) * peers
    return pl.pallas_call(
        functools.partial(gather_kernel, outer, inner, members, groups, count, 2),
        out_shape=[
            jax.ShapeDtypeStruct((outer, inner, 2, x.shape[0], members * x.shape[1]), x.dtype)
            for x in blocks
        ],
        in_specs=[pl.BlockSpec(memory_space=pl.ANY)] * count,
        out_specs=[pl.BlockSpec(memory_space=pl.ANY)] * count,
        scratch_shapes=[
            pltpu.SemaphoreType.DMA((sems,)),
            pltpu.SemaphoreType.DMA((sems,)),
            pltpu.SemaphoreType.DMA((count,)),
        ],
        compiler_params=pltpu.CompilerParams(collective_id=0, has_side_effects=True),
        name="gather_blocks",
    )(*blocks)


class Channel:
    def __init__(self, place, axis, slots, total, send, recv, free):
        self.place, self.axis, self.slots, self.total = place, axis, slots, total
        self.send_sem, self.recv_sem, self.free = send, recv, free
        self.steps = range(1, place.sizes[axis])
        self.made = {}

    def before_fill(self, turn):
        if turn >= self.slots:
            for copy in self.made[turn - self.slots]:
                copy.wait_send()

    def send(self, turn, pairs):
        slot = turn % self.slots
        self.made[turn] = []
        for step, (src, dst) in zip(self.steps, pairs):
            if turn >= self.slots:
                pl.semaphore_wait(self.free.at[step - 1], 1)
            copy = pltpu.make_async_remote_copy(
                src_ref=src,
                dst_ref=dst,
                send_sem=self.send_sem.at[slot, step - 1],
                recv_sem=self.recv_sem.at[slot, step - 1],
                device_id=self.place.device(self.axis, step),
                device_id_type=MESH,
            )
            copy.start()
            self.made[turn].append(copy)

    def receive(self, turn):
        for copy in self.made[turn]:
            copy.wait_recv()

    def consumed(self, turn):
        if turn + self.slots < self.total:
            for step in self.steps:
                pl.semaphore_signal(
                    self.free.at[step - 1],
                    inc=1,
                    device_id=self.place.device(self.axis, -step),
                    device_id_type=MESH,
                )

    def drain(self):
        for turn in range(max(0, self.total - self.slots), self.total):
            for copy in self.made[turn]:
                copy.wait_send()


def reduce_kernel(outer, inner, members, rows, halves, groups, arrays, lags, *refs):
    refs = list(refs)

    def take(number):
        taken = refs[:number]
        del refs[:number]
        return taken

    (small_in,) = take(1)
    lefts = take(arrays)
    rights = take(arrays)
    outs = take(arrays)
    small_out, square_out = take(2)
    right_buf, right_sem = take(2)
    sent0, got0, own0 = take(3)
    sent1a, got1a, keep1a, sent1b, got1b, keep1b = take(6)
    sent2a, got2a, sent2b, got2b, keep2 = take(5)
    sent3, got3 = take(2)
    sems = [take(3) for _ in range(6)]
    small_bufs = take(4)
    square_bufs = take(4)
    tiny_send, tiny_recv = take(2)

    place = Place(outer, inner, members)
    a, b, c, m = (place.at[axis] for axis in "abcm")
    total = len(groups)
    top, low_rows = halves
    lag1, lag2, lag3, lag4 = lags
    slots = (2, lag2 - lag1, lag3 - lag2, lag4 - lag3)
    chan0 = Channel(place, "c", slots[0], total, *sems[0])
    chan1a = Channel(place, "a", slots[1], total, *sems[1])
    chan1b = Channel(place, "b", slots[1], total, *sems[2])
    chan2a = Channel(place, "b", slots[2], total, *sems[3])
    chan2b = Channel(place, "a", slots[2], total, *sems[4])
    chan3 = Channel(place, "m", slots[3], total, *sems[5])
    channels = [chan0, chan1a, chan2a, chan3]
    if low_rows:
        channels += [chan1b, chan2b]

    def each_member(body):
        def step(i, unused):
            body(i)
            return 0

        lax.fori_loop(0, members, step, 0)

    def fetch(turn):
        i, first, width = groups[turn]
        block = rights[i].shape[1] // members
        depth = rights[i].shape[0]
        return [
            pltpu.make_async_copy(
                rights[i].at[:, pl.ds(k * block + first, width)],
                right_buf.at[turn % 2, k, pl.ds(0, depth), pl.ds(0, width)],
                right_sem.at[turn % 2, k],
            )
            for k in range(members)
        ]

    def product(turn, half, k):
        i, first, width = groups[turn]
        depth = rights[i].shape[0]
        return jnp.dot(
            lefts[i][half],
            right_buf[turn % 2, k, pl.ds(0, depth), pl.ds(0, width)],
            preferred_element_type=jnp.float32,
        ).reshape(outer, inner, rows, width)

    def make(turn):
        i, first, width = groups[turn]
        cols = pl.ds(0, width)
        slot = turn % 2
        for copy in fetch(turn):
            copy.wait()
        if turn + 1 < total:
            for copy in fetch(turn + 1):
                copy.start()
        chan0.before_fill(turn)

        def fill(k):
            sent0[slot, k, :, :, :, cols] = product(turn, 1 - c, k).astype(jnp.bfloat16)

        each_member(fill)
        chan0.send(
            turn, [(sent0.at[slot, :, :, :, :, cols], got0.at[slot, :, :, :, :, cols])]
        )

        def fill_own(k):
            own0[slot, k, :, :, :, cols] = product(turn, c, k)

        each_member(fill_own)

    def stage_one(turn):
        i, first, width = groups[turn]
        cols = pl.ds(0, width)
        old, new = turn % 2, turn % slots[1]
        upper, lower = pl.ds(0, top), pl.ds(top, low_rows)
        chan1a.before_fill(turn)
        if low_rows:
            chan1b.before_fill(turn)
        chan0.receive(turn)

        def body(k):
            for step in range(outer):
                part = place.shifted("a", step)
                summed = own0[old, k, part, :, upper, cols] + got0[
                    old, k, part, :, upper, cols
                ].astype(jnp.float32)
                if step:
                    sent1a[new, step - 1, k, :, :, cols] = summed.astype(jnp.bfloat16)
                else:
                    keep1a[new, k, :, :, cols] = summed
            if low_rows:
                for step in range(inner):
                    part = place.shifted("b", step)
                    summed = own0[old, k, :, part, lower, cols] + got0[
                        old, k, :, part, lower, cols
                    ].astype(jnp.float32)
                    if step:
                        sent1b[new, step - 1, k, :, :, cols] = summed.astype(jnp.bfloat16)
                    else:
                        keep1b[new, k, :, :, cols] = summed

        each_member(body)
        chan0.consumed(turn)
        chan1a.send(
            turn,
            [
                (sent1a.at[new, j, :, :, :, cols], got1a.at[new, j, :, :, :, cols])
                for j in range(outer - 1)
            ],
        )
        if low_rows:
            chan1b.send(
                turn,
                [
                    (sent1b.at[new, j, :, :, :, cols], got1b.at[new, j, :, :, :, cols])
                    for j in range(inner - 1)
                ],
            )

    def stage_two(turn):
        i, first, width = groups[turn]
        cols = pl.ds(0, width)
        old, new = turn % slots[1], turn % slots[2]
        chan2a.before_fill(turn)
        if low_rows:
            chan2b.before_fill(turn)
        chan1a.receive(turn)
        if low_rows:
            chan1b.receive(turn)

        def body(k):
            for step in range(inner):
                part = place.shifted("b", step)
                summed = keep1a[old, k, part, :, cols]
                for j in range(outer - 1):
                    summed += got1a[old, j, k, part, :, cols].astype(jnp.float32)
                if step:
                    sent2a[new, step - 1, k, :, cols] = summed.astype(jnp.bfloat16)
                else:
                    keep2[new, k, pl.ds(0, top), cols] = summed
            if low_rows:
                for step in range(outer):
                    part = place.shifted("a", step)
                    summed = keep1b[old, k, part, :, cols]
                    for j in range(inner - 1):
                        summed += got1b[old, j, k, part, :, cols].astype(jnp.float32)
                    if step:
                        sent2b[new, step - 1, k, :, cols] = summed.astype(jnp.bfloat16)
                    else:
                        keep2[new, k, pl.ds(top, low_rows), cols] = summed

        each_member(body)
        chan1a.consumed(turn)
        if low_rows:
            chan1b.consumed(turn)
        chan2a.send(
            turn,
            [
                (sent2a.at[new, j, :, :, cols], got2a.at[new, j, :, :, cols])
                for j in range(inner - 1)
            ],
        )
        if low_rows:
            chan2b.send(
                turn,
                [
                    (sent2b.at[new, j, :, :, cols], got2b.at[new, j, :, :, cols])
                    for j in range(outer - 1)
                ],
            )

    def stage_three(turn):
        i, first, width = groups[turn]
        cols = pl.ds(0, width)
        old, new = turn % slots[2], turn % slots[3]
        chan3.before_fill(turn)
        chan2a.receive(turn)
        if low_rows:
            chan2b.receive(turn)

        def body(k):
            summed = keep2[old, k, pl.ds(0, top), cols]
            for j in range(inner - 1):
                summed += got2a[old, j, k, :, cols].astype(jnp.float32)
            sent3[new, k, pl.ds(0, top), cols] = summed
            if low_rows:
                summed = keep2[old, k, pl.ds(top, low_rows), cols]
                for j in range(outer - 1):
                    summed += got2b[old, j, k, :, cols].astype(jnp.float32)
                sent3[new, k, pl.ds(top, low_rows), cols] = summed

        each_member(body)
        chan2a.consumed(turn)
        if low_rows:
            chan2b.consumed(turn)
        chan3.send(
            turn,
            [
                (sent3.at[new, place.shifted("m", j + 1), :, cols], got3.at[new, j, :, cols])
                for j in range(members - 1)
            ],
        )

    def stage_four(turn):
        i, first, width = groups[turn]
        cols = pl.ds(0, width)
        old = turn % slots[3]
        chan3.receive(turn)
        summed = sent3[old, m, :, cols]
        for j in range(members - 1):
            summed += got3[old, j, :, cols]
        outs[i][:, pl.ds(first, width)] = summed
        chan3.consumed(turn)

    tiny_used = [0]
    tiny_made = []

    def spread(buf, axis):
        made = []
        entry = buf.at[place.at[axis]]
        for step in range(1, place.sizes[axis]):
            k = tiny_used[0]
            tiny_used[0] += 1
            copy = pltpu.make_async_remote_copy(
                src_ref=entry,
                dst_ref=entry,
                send_sem=tiny_send.at[k],
                recv_sem=tiny_recv.at[k],
                device_id=place.device(axis, step),
                device_id_type=MESH,
            )
            copy.start()
            made.append(copy)
        tiny_made.extend(made)
        return made

    def sum_entries(buf, made):
        for copy in made:
            copy.wait_recv()
        summed = buf[0]
        for k in range(1, buf.shape[0]):
            summed += buf[k]
        return summed

    place.enter()
    for copy in fetch(0):
        copy.start()
    small_made = [None] * 4
    for tick in range(total + lag4):
        if lag4 <= tick:
            stage_four(tick - lag4)
        if 0 <= tick - lag3 < total:
            stage_three(tick - lag3)
        if 0 <= tick - lag2 < total:
            stage_two(tick - lag2)
        if 0 <= tick - lag1 < total:
            stage_one(tick - lag1)
        if tick < total:
            make(tick)
        if tick in (1, 3, 5, 7, 9):
            hop = (tick - 1) // 2
            value = small_in[...] if hop == 0 else sum_entries(small_bufs[hop - 1], small_made[hop - 1])
            if hop == 4:
                small_out[...] = value
            else:
                axis = "cabm"[hop]
                small_bufs[hop][place.at[axis]] = value
                small_made[hop] = spread(small_bufs[hop], axis)
    for channel in channels:
        channel.drain()
    value = jnp.zeros((8, 128), jnp.float32)
    for i in range(arrays):
        block = outs[i][...]
        value += jnp.sum((block * block).reshape(-1, 8, 128), 0) if block.shape[1] == 128 else sum_tiles(block)
    for hop, axis in enumerate("cabm"):
        square_bufs[hop][place.at[axis]] = value
        value = sum_entries(square_bufs[hop], spread(square_bufs[hop], axis))
    square_out[...] = value
    for copy in tiny_made:
        copy.wait_send()


def sum_tiles(block):
    squares = block * block
    folded = squares[:8]
    for first in range(8, block.shape[0], 8):
        folded += squares[first : first + 8]
    total = folded[:, :128]
    for first in range(128, block.shape[1], 128):
        total += folded[:, first : first + 128]
    return total


def reduce_products(pairs, small, ndp, members):
    outer, inner = factor(ndp)
    per_device = pairs[0][0].shape[1] // ndp
    rows = -(-per_device // 16) * 16
    both = outer * inner
    wide = both * rows <= 400
    halves = (rows // 2, rows // 2) if rows % 32 == 0 else (rows, 0)
    top, low_rows = halves
    low_shape = max(low_rows, 16)
    lags = (1, 3, 5, 7)
    slots = (2, 2, 2, 2)
    lefts, rights, groups, outs = [], [], [], []
    for i, (x, y) in enumerate(pairs):
        depth = x.shape[0]
        turned = x.T.reshape(both, 2, per_device, depth)
        turned = jnp.pad(turned, ((0, 0), (0, 0), (0, rows - per_device), (0, 0)))
        lefts.append(turned.transpose(1, 0, 2, 3).reshape(2, both * rows, depth))
        rights.append(y)
        block = y.shape[1] // members
        width = (512 if block % 512 == 0 else 384) if wide else 256
        groups += [(i, first, width) for first in range(0, block, width)]
        outs.append(jax.ShapeDtypeStruct((rows, block), jnp.float32))
    most = max(width for _, _, width in groups)
    deepest = max(y.shape[0] for y in rights)
    count = len(pairs)
    small_shape = small.shape
    bf, f4 = jnp.bfloat16, jnp.float32
    mem = pltpu.VMEM
    scratch = [
        mem((2, members, deepest, most), bf),
        pltpu.SemaphoreType.DMA((2, members)),
        mem((slots[0], members, outer, inner, rows, most), bf),
        mem((slots[0], members, outer, inner, rows, most), bf),
        mem((2, members, outer, inner, rows, most), f4),
        mem((slots[1], outer - 1, members, inner, top, most), bf),
        mem((slots[1], outer - 1, members, inner, top, most), bf),
        mem((slots[1], members, inner, top, most), f4),
        mem((slots[1], inner - 1, members, outer, low_shape, most), bf),
        mem((slots[1], inner - 1, members, outer, low_shape, most), bf),
        mem((slots[1], members, outer, low_shape, most), f4),
        mem((slots[2], inner - 1, members, top, most), bf),
        mem((slots[2], inner - 1, members, top, most), bf),
        mem((slots[2], outer - 1, members, low_shape, most), bf),
        mem((slots[2], outer - 1, members, low_shape, most), bf),
        mem((slots[2], members, rows, most), f4),
        mem((slots[3], members, rows, most), f4),
        mem((slots[3], members - 1, rows, most), f4),
    ]
    for depth, size in zip((0, 1, 1, 2, 2, 3), (2, outer, inner, inner, outer, members)):
        scratch += [
            pltpu.SemaphoreType.DMA((slots[depth], size - 1)),
            pltpu.SemaphoreType.DMA((slots[depth], size - 1)),
            pltpu.SemaphoreType.REGULAR((size - 1,)),
        ]
    sizes = (2, outer, inner, members)
    scratch += [mem((size,) + small_shape, f4) for size in sizes]
    scratch += [mem((size, 8, 128), f4) for size in sizes]
    tiny = 2 * sum(size - 1 for size in sizes)
    scratch += [pltpu.SemaphoreType.DMA((tiny,)), pltpu.SemaphoreType.DMA((tiny,))]
    vmem = pl.BlockSpec(memory_space=pltpu.VMEM)
    results = pl.pallas_call(
        functools.partial(
            reduce_kernel, outer, inner, members, rows, halves, groups, count, lags
        ),
        out_shape=outs
        + [jax.ShapeDtypeStruct(small_shape, f4), jax.ShapeDtypeStruct((8, 128), f4)],
        in_specs=[vmem] * (1 + count) + [pl.BlockSpec(memory_space=pl.ANY)] * count,
        out_specs=[vmem] * (count + 2),
        scratch_shapes=scratch,
        compiler_params=pltpu.CompilerParams(
            collective_id=1, has_side_effects=True, vmem_limit_bytes=62 * 2**20
        ),
        name="reduce_products",
    )(small, *lefts, *rights)
    return [block[:per_device] for block in results[:count]], results[count], results[count + 1]


def local(members, ndp, *args):
    (
        qkv_weight, qkv_first, qkv_second,
        out_weight, out_first, out_second,
        up_weight, up_first, up_second,
        down_weight, down_first, down_second,
        code_table, table_first, table_second,
        small_params, small_first, small_second,
        patch_codes, masked_pos, masked_count,
    ) = args
    bf, f4 = jnp.bfloat16, jnp.float32
    member = lax.axis_index("mp")
    images = patch_codes.shape[0] // members
    rows_all = images * SEQ
    depth = -(-rows_all // 16) * 16
    heads_part = H // members
    width_part = D // members
    score_scale = DH ** (-0.5)
    axis_hot = offset_table()
    vectors, fc_bias, rel_tables, special = unpack_small(small_params)

    blocks = []
    count_here = jnp.full((8, 128), jnp.sum(masked_count).astype(f4))
    for l in range(LAYERS):
        blocks.append(
            jnp.concatenate(
                [qkv_weight[l, 0], qkv_weight[l, 1], qkv_weight[l, 2], out_weight[l].T], 1
            ).astype(bf)
        )
        blocks.append(up_weight[l].astype(bf))
        blocks.append(down_weight[l].T.astype(bf))
    blocks = [blocks[0], code_table.T.astype(bf)] + blocks[1:] + [count_here]
    gathered = list(gather_blocks(blocks, ndp, members))
    counts_all = gathered.pop()
    mats = [g.reshape(D, g.shape[-1]) for g in gathered]
    table = mats.pop(1)
    layer_mats = [mats[3 * l : 3 * l + 3] for l in range(LAYERS)]
    count_total = jnp.sum(counts_all.reshape(ndp, 8, members * 128)[:, 0, 0])
    inverse_total = jnp.ones((), f4) / count_total

    def mine(values):
        return lax.dynamic_slice_in_dim(values, member * images, images, 0)

    image_codes = mine(patch_codes)
    masked_spots = mine(masked_pos)
    counts = mine(masked_count)
    valid_slots = jnp.arange(MAXM)[None, :] < counts[:, None]
    hidden_patch = jnp.any(
        (masked_spots[:, :, None] == jnp.arange(PATCH)[None, None, :]) & valid_slots[:, :, None], 1
    )
    masked_rows = jnp.concatenate([jnp.zeros((images, 1), jnp.bool_), hidden_patch], 1).reshape(-1)
    cls_rows = jnp.arange(rows_all) % SEQ == 0
    seen_rows = jnp.logical_not(masked_rows | cls_rows)
    row_codes = jnp.concatenate([jnp.zeros((images, 1), jnp.int32), image_codes], 1).reshape(-1)
    code_hot = (seen_rows[:, None] & (row_codes[:, None] == jnp.arange(V)[None, :])).astype(bf)
    pick_hot = (masked_spots[:, :, None] + 1 == jnp.arange(SEQ)[None, None, :]).astype(f4)
    targets = jnp.take_along_axis(image_codes, masked_spots, 1).reshape(-1)
    valid_float = valid_slots.reshape(-1).astype(f4)
    row_weight = valid_float * inverse_total

    def by_rows(x, w):
        return lax.dot_general(x, w, (((1,), (1,)), ((), ())), preferred_element_type=f4)

    def dot(x, w):
        return jnp.dot(x, w, preferred_element_type=f4)

    def split_heads(values):
        return values.reshape(images, SEQ, H, DH)

    def out_part(attn_mat):
        return attn_mat.reshape(D, members, 4 * width_part)[:, :, 3 * width_part :].reshape(D, D)

    embedded = by_rows(code_hot, table)
    fallback = jnp.where(cls_rows[:, None], special[0], special[1])
    x = jnp.where(seen_rows[:, None], embedded, fallback)
    caches = []
    for l in range(LAYERS):
        attn_mat, up_mat, down_mat = layer_mats[l]
        vec = vectors[l]
        attn_in = layer_norm(x, vec[0], vec[1]).astype(bf)
        projected = dot(attn_in, attn_mat).reshape(rows_all, members, 4, width_part)
        query_rows = (projected[:, :, 0].reshape(rows_all, D) + vec[2]).astype(bf)
        key_rows = projected[:, :, 1].reshape(rows_all, D).astype(bf)
        value_rows = (projected[:, :, 2].reshape(rows_all, D) + vec[3]).astype(bf)
        rel_bias = bias_block(rel_tables[l], axis_hot)
        raw_scores = jnp.einsum(
            "bqhd,bkhd->bhqk", split_heads(query_rows), split_heads(key_rows),
            preferred_element_type=f4,
        )
        attn_probs = softmax_rows(raw_scores * score_scale + rel_bias[None])
        mixed = (
            jnp.einsum(
                "bhqk,bkhd->bqhd", attn_probs.astype(bf), split_heads(value_rows),
                preferred_element_type=f4,
            )
            .reshape(rows_all, D)
            .astype(bf)
        )
        out_mat = out_part(attn_mat)
        attn_out = by_rows(mixed, out_mat) + vec[4]
        x_mid = x + vec[5] * attn_out
        mlp_in = layer_norm(x_mid, vec[6], vec[7]).astype(bf)
        pre_act = dot(mlp_in, up_mat) + fc_bias[l]
        activated = exact_gelu(pre_act).astype(bf)
        mlp_out = by_rows(activated, down_mat) + vec[8]
        caches.append(
            (x, attn_in, query_rows, key_rows, value_rows, attn_probs, mixed, out_mat, attn_out,
             x_mid, mlp_in, pre_act, activated, mlp_out)
        )
        x = x_mid + vec[9] * mlp_out

    last_normed = layer_norm(x, special[2], special[3]).astype(bf)
    picked = (
        jnp.einsum(
            "bst,btd->bsd", pick_hot.astype(bf), last_normed.reshape(images, SEQ, D),
            preferred_element_type=f4,
        )
        .astype(bf)
        .reshape(images * MAXM, D)
    )
    logits = dot(picked, table)
    target_hits = jnp.arange(V)[None, :] == targets[:, None]
    target_logit = jnp.sum(jnp.where(target_hits, logits, 0.0), 1)
    highest = jnp.max(logits, 1)
    exp_sums = jnp.sum(jnp.exp(logits - highest[:, None]), 1)
    log_total = highest + jnp.log(exp_sums)
    loss_part = jnp.sum((log_total - target_logit) * valid_float)
    d_logits = (
        (jnp.exp(logits - log_total[:, None]) - target_hits.astype(f4)) * row_weight[:, None]
    ).astype(bf)
    d_picked = by_rows(d_logits, table)
    d_normed = jnp.einsum(
        "bst,bsd->btd", pick_hot, d_picked.reshape(images, MAXM, D), precision=HIGHEST
    ).reshape(rows_all, D)
    unused, pullback = jax.vjp(layer_norm, x, special[2], special[3])
    upstream, d_gain, d_shift = pullback(d_normed)

    def padded(values):
        return jnp.pad(values, ((0, depth - rows_all), (0, 0)))

    pairs = [None] * LAYERS
    vec_grads, fc_grads, rel_grads = [None] * LAYERS, [None] * LAYERS, [None] * LAYERS
    for l in reversed(range(LAYERS)):
        attn_mat, up_mat, down_mat = layer_mats[l]
        (x_in, attn_in, query_rows, key_rows, value_rows, attn_probs, mixed, out_mat, attn_out,
         x_mid, mlp_in, pre_act, activated, mlp_out) = caches[l]
        vec = vectors[l]
        g_mlp = (vec[9] * upstream).astype(bf)
        d_gamma2 = jnp.sum(upstream * mlp_out, 0)
        d_down_bias = jnp.sum(g_mlp.astype(f4), 0)
        d_act = dot(g_mlp, down_mat)
        unused, pullback = jax.vjp(exact_gelu, pre_act)
        d_pre = pullback(d_act)[0].astype(bf)
        fc_grads[l] = jnp.sum(d_pre.astype(f4), 0)
        d_norm2 = by_rows(d_pre, up_mat)
        unused, pullback = jax.vjp(layer_norm, x_mid, vec[6], vec[7])
        d_mid, d_gain2, d_shift2 = pullback(d_norm2)
        d_mid = d_mid + upstream
        g_attn = (vec[5] * d_mid).astype(bf)
        d_gamma1 = jnp.sum(d_mid * attn_out, 0)
        d_out_bias = jnp.sum(g_attn.astype(f4), 0)
        d_mixed = split_heads(dot(g_attn, out_mat).astype(bf))
        d_probs = jnp.einsum(
            "bqhd,bkhd->bhqk", d_mixed, split_heads(value_rows), preferred_element_type=f4
        )
        d_value = jnp.einsum(
            "bhqk,bqhd->bkhd", attn_probs.astype(bf), d_mixed, preferred_element_type=f4
        ).astype(bf)
        d_scores = (
            attn_probs * (d_probs - jnp.sum(attn_probs * d_probs, -1, keepdims=True))
        ).astype(bf)
        d_query = (
            jnp.einsum(
                "bhqk,bkhd->bqhd", d_scores, split_heads(key_rows), preferred_element_type=f4
            )
            * score_scale
        ).astype(bf)
        d_key = (
            jnp.einsum(
                "bhqk,bqhd->bkhd", d_scores, split_heads(query_rows), preferred_element_type=f4
            )
            * score_scale
        ).astype(bf)
        rel_grads[l] = bias_grad(jnp.sum(d_scores.astype(f4), 0), axis_hot)

        def parts(values):
            return values.reshape(rows_all, members, 1, width_part)

        d_cat = jnp.concatenate(
            [parts(d_query), parts(d_key), parts(d_value), jnp.zeros_like(parts(d_value))], 2
        ).reshape(rows_all, 4 * D)
        mixed_cat = jnp.pad(parts(mixed), ((0, 0), (0, 0), (3, 0), (0, 0))).reshape(rows_all, 4 * D)
        d_norm1 = by_rows(d_cat, attn_mat)
        unused, pullback = jax.vjp(layer_norm, x_in, vec[0], vec[1])
        d_input, d_gain1, d_shift1 = pullback(d_norm1)
        vec_grads[l] = jnp.stack(
            [
                d_gain1, d_shift1,
                jnp.sum(d_query.reshape(rows_all, D).astype(f4), 0),
                jnp.sum(d_value.reshape(rows_all, D).astype(f4), 0),
                d_out_bias, d_gamma1, d_gain2, d_shift2, d_down_bias, d_gamma2,
            ]
        )
        pairs[l] = [
            (
                jnp.concatenate([padded(attn_in), padded(g_attn)], 0),
                jnp.concatenate([padded(d_cat), padded(mixed_cat)], 0),
            ),
            (padded(mlp_in), padded(d_pre)),
            (padded(g_mlp), padded(activated)),
        ]
        upstream = d_input + d_mid
    d_cls = jnp.sum(jnp.where(cls_rows[:, None], upstream, 0.0), 0)
    d_mask = jnp.sum(jnp.where(masked_rows[:, None], upstream, 0.0), 0)
    seen_grad = jnp.where(seen_rows[:, None], upstream, 0.0).astype(bf)
    table_depth = images * MAXM + rows_all
    table_pad = ((0, -table_depth % 16), (0, 0))
    table_pair = (
        jnp.pad(jnp.concatenate([picked, seen_grad], 0), table_pad),
        jnp.pad(jnp.concatenate([d_logits, code_hot], 0), table_pad),
    )
    small_grad = pack_small(
        jnp.stack(vec_grads), jnp.stack(fc_grads), jnp.stack(rel_grads),
        jnp.stack([d_cls, d_mask, d_gain, d_shift]),
    )
    small_size = small_grad.shape[0]
    packed = jnp.concatenate([small_grad, loss_part[None]])
    packed = jnp.pad(packed, (0, -packed.shape[0] % 1024)).reshape(-1, 128)

    all_pairs = [table_pair] + [pair for l in reversed(range(LAYERS)) for pair in pairs[l]]
    grads, small_sum, squares = reduce_products(all_pairs, packed, ndp, members)
    grad_table = grads[0].T
    by_layer = [grads[1 + 3 * (LAYERS - 1 - l) :][:3] for l in range(LAYERS)]
    grad_qkv = jnp.stack(
        [
            jnp.stack([g[0][:, j * width_part : (j + 1) * width_part] for j in range(3)])
            for g in by_layer
        ]
    )
    grad_out = jnp.stack([g[0][:, 3 * width_part :].T for g in by_layer])
    grad_up = jnp.stack([g[1] for g in by_layer])
    grad_down = jnp.stack([g[2].T for g in by_layer])
    small_sum = small_sum.reshape(-1)
    grad_small = small_sum[:small_size]
    loss_total = small_sum[small_size]
    grad_norm = jnp.sqrt(jnp.sum(squares) + jnp.sum(grad_small * grad_small))
    factor_clip = jnp.minimum(1.0, CLIP_NORM / (grad_norm + 1e-06))
    results = ()
    for weight, one, two, grad, decay in (
        (qkv_weight, qkv_first, qkv_second, grad_qkv, WEIGHT_DECAY),
        (out_weight, out_first, out_second, grad_out, WEIGHT_DECAY),
        (up_weight, up_first, up_second, grad_up, WEIGHT_DECAY),
        (down_weight, down_first, down_second, grad_down, WEIGHT_DECAY),
        (code_table, table_first, table_second, grad_table, WEIGHT_DECAY),
        (small_params, small_first, small_second, grad_small, 0.0),
    ):
        results += adam_update(weight, one, two, grad, factor_clip, decay)
    return results + (loss_total, count_total, grad_norm)


def solution(mesh):
    in_specs = (
        P(None, None, "dp", "mp"),
        P(None, None, "dp", "mp"),
        P(None, None, "dp", "mp"),
        P(None, "mp", "dp"),
        P(None, "mp", "dp"),
        P(None, "mp", "dp"),
        P(None, "dp", "mp"),
        P(None, "dp", "mp"),
        P(None, "dp", "mp"),
        P(None, "mp", "dp"),
        P(None, "mp", "dp"),
        P(None, "mp", "dp"),
        P("mp", "dp"),
        P("mp", "dp"),
        P("mp", "dp"),
        P(),
        P(),
        P(),
        P("dp", None),
        P("dp", None),
        P("dp"),
    )
    out_specs = (
        P(None, None, "dp", "mp"),
        P(None, None, "dp", "mp"),
        P(None, None, "dp", "mp"),
        P(None, "mp", "dp"),
        P(None, "mp", "dp"),
        P(None, "mp", "dp"),
        P(None, "dp", "mp"),
        P(None, "dp", "mp"),
        P(None, "dp", "mp"),
        P(None, "mp", "dp"),
        P(None, "mp", "dp"),
        P(None, "mp", "dp"),
        P("mp", "dp"),
        P("mp", "dp"),
        P("mp", "dp"),
        P(),
        P(),
        P(),
        P(),
        P(),
        P(),
    )
    body = functools.partial(local, mesh.shape["mp"], mesh.shape["dp"])
    return jax.shard_map(body, mesh=mesh, in_specs=in_specs, out_specs=out_specs, check_vma=False)
```

time: 2530 us -> 1150 us (0.45)
  blocking collectives: 980 us -> 0 us
  waiting for transfers between devices: 831 us -> 0 us
  Pallas kernels: 0 us -> 503 us
  matrix products: 262 us -> 199 us
  starting transfers between devices: 51.7 us -> 0 us
  local copies, waits for them, and re-layouts: 273 us -> 315 us
  other arithmetic: 87.7 us -> 114 us
    unnamed x10 -> x0, blocking collectives: 860 us -> none
    pallas_call x0 -> x2, Pallas kernels: none -> 503 us  [the longest x1 282 us: reduce_products(): pl.pallas_call(functools.partial(reduce_kernel, outer, inner, members, ro...]
    all_gather x25 -> x0, waiting for transfers between devices: 485 us -> none  [the longest x20 400 us: gather_rows(): return lax.all_gather(values, 'mp', axis=0, tiled=True)]
    psum x1 -> x0, waiting for transfers between devices: 125 us -> none  [local(): lax.psum(pack_small(stack_of(small_sums, 0), stack_of(small_sums, 1), sta...]
    reduce_scatter x2 -> x0, waiting for transfers between devices: 116 us -> none  [the longest x1 60.2 us: local(): lax.psum_scatter(matrix_sums[4], 'dp', scatter_dimension=1, tiled=True)]
    unnamed x54 -> x0, waiting for transfers between devices: 105 us -> none
    unnamed x863 -> x373, local copies, waits for them, and re-layouts: 140 us -> 36.2 us
    psum x3 -> x0, blocking collectives: 63.7 us -> none  [the longest x1 42.2 us: local(): lax.psum((own_squares, loss_sum * first_member), ('dp', 'mp'))]
  transfers between devices with their start and end apart: 51 -> 0, of which waited for: 31 -> 0; matrix products, arithmetic and copies ran while one was open for 12% -> 0% of each run, Pallas kernels for 0% -> 0%
where the time goes in v1:
time: 1150 us; the launch traced here: 1140 us
  Pallas kernels  503 us (44%)
  local copies, waits for them, and re-layouts  315 us (27%)
  matrix products  199 us (17%)
  other arithmetic  114 us (10%)
    pallas_call x1, Pallas kernels, reduce_products(): pl.pallas_call(functools.partial(reduce_kernel, outer, inner, members, ro...  282 us
    pallas_call x1, Pallas kernels, gather_blocks(): pl.pallas_call(functools.partial(gather_kernel, outer, inner, members, gr...  220 us
    dot_general x9, matrix products, dot(): return jnp.dot(x, w, preferred_element_type=f4)  69.4 us
    dot_general x10, matrix products, by_rows(): lax.dot_general(x, w, (((1,), (1,)), ((), ())), preferred_element_type=f4)  47.9 us
    unnamed x373, local copies, waits for them, and re-layouts  36.2 us
    reshape x2, local copies, waits for them, and re-layouts, bias_block(): jnp.einsum('hiqs,pri->hpqrs', across, axis_hot, precision=HIGHEST)  25.7 us
    reshape x2, local copies, waits for them, and re-layouts, bias_grad(): inner = score_sums[:, 1:, 1:].reshape(heads_here, GRID, GRID, GRID, GRID)  24.4 us
    dot_general x2, matrix products, bias_grad(): across = jnp.einsum('hpqrs,qsj->hprj', inner, axis_hot, precision=HIGHEST)  23.9 us

profile of v1, /device:TPU:0, one launch (start us, length us, event | category | flops | bytes accessed | tf_op | source)
XLA Modules:
  0.0 1137.8 jit_solution(4977234281533585662)
XLA Ops:
  8.2 220.2 %gather_blocks.1 = (bf16[2,2,2,96,3072]{4,3,2,1,0:T(8,128)(2,1)}, bf16[2,2,2,96,8192]{4,3,2,1,0:T(8,128)(2,1)}, bf16[2,2,2,96,3072]{4,3,2,1,0:T(8,128)(2,1)}, bf...) custom-call(bf16[96,768]{1,0:T(8,128)(2,1)} %get-tuple-element.361.r, ...), custom_call_target="tpu_custom_call" | custom-call | tf_op jit(solution)/shard_map/gather_blocks/pallas_call | solution.py:256
  232.4 11.0 fusion.147
  244.6 6.9 copy.376
  251.5 4.6 fusion.69
  270.4 4.2 fusion.61
  275.8 7.7 convolution_bitcast_fusion.1
  283.5 6.9 copy.380
  290.4 13.1 %reshape.665 = f32[12,196,196]{2,1,0:T(8,128)} reshape(f32[12,14,14,14,14]{4,3,2,1,0:T(8,128)} %copy.380) | data formatting | bytes 3687936 | tf_op jit(solution)/shard_map/reshape | solution.py:94
  311.1 9.2 fusion.148
  327.8 9.8 reshape_reshape.6
  347.8 14.3 %multiply_convert_fusion.4 = (bf16[394,3072]{1,0:T(8,128)(2,1)S(1)}, f32[394,3072]{1,0:T(8,128)}, f32[394,3072]{1,0:T(8,128)}) fusion(f32[3072]{0:T(1024)S(1)} %get-tuple-element.321, bf16[394,768]{1,0:T(8,128)(2,1)S(1)} %add_convert_fusion.5, bf16[768,3072]{1,0:T(8,128)(2,1)S(1)} %bitcast.392), kind=kOutput, calls=%fused_computation.53 | convolution fusion | flops 1939009536 | bytes 17439744 | tf_op jit(solution)/shard_map/dot_general | solution.py:779
  366.1 6.9 copy.386
  372.9 4.6 fusion.67
  391.0 4.3 fusion.64
  396.4 7.7 convolution_bitcast_fusion
  404.1 6.9 copy.390
  411.0 12.7 %reshape.671 = f32[12,196,196]{2,1,0:T(8,128)} reshape(f32[12,14,14,14,14]{4,3,2,1,0:T(8,128)} %copy.390) | data formatting | bytes 3687936 | tf_op jit(solution)/shard_map/reshape | solution.py:94
  431.5 9.2 fusion.149
  448.2 9.8 reshape_reshape.7
  466.8 15.7 %multiply_convert_fusion.3 = (bf16[394,3072]{1,0:T(8,128)(2,1)S(1)}, f32[394,3072]{1,0:T(8,128)}, f32[394,3072]{1,0:T(8,128)}) fusion(f32[3072]{0:T(1024)S(1)} %get-tuple-element.320, bf16[394,768]{1,0:T(8,128)(2,1)S(1)} %add_convert_fusion.3, bf16[768,3072]{1,0:T(8,128)(2,1)} %bitcast.400), kind=kOutput, calls=%fused_computation.38 | convolution fusion | flops 1939009536 | bytes 17439744 | tf_op jit(solution)/shard_map/dot_general | solution.py:779
  490.8 8.9 fusion.150
  506.5 3.9 multiply_convert_fusion
  512.6 9.7 fusion.152
  528.2 9.2 convert_reduce_fusion.2
  554.0 5.3 convert_reduce_fusion
  566.5 4.0 convert_reduce_fusion.4
  574.8 4.8 copy.406
  579.7 7.5 reshape.684
  587.3 6.1 multiply_reduce_fusion.13
  596.2 8.9 convert_reduce_fusion.3
  622.8 5.2 convert_reduce_fusion.1
  634.5 4.0 convert_reduce_fusion.6
  642.0 7.2 copy.417
  649.2 5.9 reshape.689
  657.6 4.0 copy.474
  665.4 5.9 reshape.724
  671.3 5.7 fusion.15.refs_12_
  677.5 4.1 copy.473
  685.3 6.0 reshape.723
  691.2 5.8 fusion.14.refs_9_
  702.2 5.3 multiply_reduce_fusion.3
  719.7 11.7 %reshape.700 = f32[12,14,14,14,14]{4,3,2,1,0:T(8,128)} reshape(f32[12,196,196]{2,1,0:T(8,128)S(1)} %copy.418) | data formatting | bytes 3687936 | tf_op jit(solution)/shard_map/reshape | solution.py:113
  731.4 12.0 %convolution_bitcast_fusion.3 = f32[12,14,14,27]{3,2,1,0:T(8,128)S(1)} fusion(f32[12,14,14,14,14]{4,3,2,1,0:T(8,128)} %reshape.700, s32[14,14]{1,0:T(8,128)S(1)} %copy-done.76), kind=kOutput, calls=%fused_computation.112 | convolution fusion | flops 149366704 | bytes 2098768 | tf_op jit(solution)/shard_map/hpqrs,qsj->hprj/dot_general | solution.py:114
  753.5 12.7 %reshape.702 = f32[12,14,14,14,14]{4,3,2,1,0:T(8,128)} reshape(f32[12,196,196]{2,1,0:T(8,128)} %copy.422) | data formatting | bytes 3687936 | tf_op jit(solution)/shard_map/reshape | solution.py:113
  766.2 12.0 %convolution_bitcast_fusion.2 = f32[12,14,14,27]{3,2,1,0:T(8,128)S(1)} fusion(f32[12,14,14,14,14]{4,3,2,1,0:T(8,128)} %reshape.702, s32[14,14]{1,0:T(8,128)S(1)} %copy-done.76), kind=kOutput, calls=%fused_computation.111 | convolution fusion | flops 149366704 | bytes 2098768 | tf_op jit(solution)/shard_map/hpqrs,qsj->hprj/dot_general | solution.py:114
  794.9 6.1 fusion.3
  801.0 8.1 pad_maximum_fusion.refs_8_
  832.3 282.4 %reduce_products.1 = (f32[96,2048]{1,0:T(8,128)}, f32[96,768]{1,0:T(8,128)}, f32[96,768]{1,0:T(8,128)}, f32[96,768]{1,0:T(8,128)}, f32[96,768]{1,0:T(8,128)}, /*...) custom-call(f32[336,128]{1,0:T(8,128)} %pad_bitcast_fusion.4.refs_0_, ...), custom_call_target="tpu_custom_call" | custom-call | tf_op jit(solution)/shard_map/reduce_products/pallas_call | solution.py:698
  (633 shorter events, 272.2 us)
Async XLA Ops:
  0.7 230.3 %copy-start = (s32[8,196]{1,0:T(8,128)S(1)}, s32[8,196]{1,0:T(8,128)}, u32[]{:S(2)}) copy-start(s32[8,196]{1,0:T(8,128)} %param.39) | copy-start | bytes 18820
  4.0 227.7 %copy-start.79 = (f32[42144]{0:T(1024)S(1)}, f32[42144]{0:T(1024)}, u32[]{:S(2)}) copy-start(f32[42144]{0:T(1024)} %param.36) | copy-start | bytes 505732
  230.9 12.4 %copy-start.158 = (pred[394]{0:T(512)(128)(4,1)}, pred[394]{0:T(512)(128)(4,1)S(1)}, u32[]{:S(2)}) copy-start(pred[394]{0:T(512)(128)(4,1)S(1)} %get-tuple-element.364) | copy-start | bytes 1186
  230.9 12.4 %copy-start.165 = (pred[394]{0:T(512)(128)(4,1)}, pred[394]{0:T(512)(128)(4,1)S(1)}, u32[]{:S(2)}) copy-start(pred[394]{0:T(512)(128)(4,1)S(1)} %get-tuple-element.363) | copy-start | bytes 1186
  231.7 11.7 %copy-start.147 = (s32[394]{0:T(512)}, s32[394]{0:T(512)S(1)}, u32[]{:S(2)}) copy-start(s32[394]{0:T(512)S(1)} %eq.130) | copy-start | bytes 4732
  232.4 12.0 %copy-start.106 = (f32[768]{0:T(1024)}, f32[768]{0:T(1024)S(1)}, u32[]{:S(2)}) copy-start(f32[768]{0:T(1024)S(1)} %get-tuple-element.317) | copy-start | bytes 9220
  243.4 100.6 %copy-start.10 = (f32[394,768]{1,0:T(8,128)}, f32[394,768]{1,0:T(8,128)S(1)}, u32[]{:S(2)}) copy-start(f32[394,768]{1,0:T(8,128)S(1)} %get-tuple-element.330) | copy-start | bytes 3631108
  262.6 12.0 %copy-start.18 = (f32[2,197,12,64]{1,0,3,2:T(2,128)}, f32[2,197,12,64]{1,0,3,2:T(2,128)S(1)}, u32[]{:S(2)}) copy-start(f32[2,197,12,64]{1,0,3,2:T(2,128)S(1)} %reshape_squeeze.14) | copy-start | bytes 3631108
  269.7 74.3 %copy-start.104 = (f32[768]{0:T(1024)}, f32[768]{0:T(1024)S(1)}, u32[]{:S(2)}) copy-start(f32[768]{0:T(1024)S(1)} %get-tuple-element.313) | copy-start | bytes 9220
  269.7 76.5 %copy-start.108 = (f32[768]{0:T(1024)}, f32[768]{0:T(1024)S(1)}, u32[]{:S(2)}) copy-start(f32[768]{0:T(1024)S(1)} %get-tuple-element.310) | copy-start | bytes 9220
  269.7 92.5 %copy-start.131 = (f32[768]{0:T(1024)}, f32[768]{0:T(1024)S(1)}, u32[]{:S(2)}) copy-start(f32[768]{0:T(1024)S(1)} %get-tuple-element.308) | copy-start | bytes 9220
  269.7 96.0 %copy-start.110 = (f32[768]{0:T(1024)}, f32[768]{0:T(1024)S(1)}, u32[]{:S(2)}) copy-start(f32[768]{0:T(1024)S(1)} %get-tuple-element.306) | copy-start | bytes 9220
  274.6 121.8 %copy-start.75 = (s32[14,14]{1,0:T(8,128)}, s32[14,14]{1,0:T(8,128)S(1)}, u32[]{:S(2)}) copy-start(s32[14,14]{1,0:T(8,128)S(1)} %subtract_add_fusion) | copy-start | bytes 2356
  311.1 9.2 copy-start.30
  327.3 10.2 copy-start.25
  344.0 18.2 %slice-start.4 = ((s8[4718592]{0:T(1024)(128)(4,1)}), s8[4194304]{0:T(1024)(128)(4,1)S(1)}, s32[]{:S(2)}) async-start(s8[4718592]{0:T(1024)(128)(4,1)} %bitcast.397), calls=%async_computation.4 | async-start | bytes 8388608
  345.8 16.4 %copy-start.6 = (f32[394,768]{1,0:T(8,128)}, f32[394,768]{1,0:T(8,128)S(1)}, u32[]{:S(2)}) copy-start(f32[394,768]{1,0:T(8,128)S(1)} %get-tuple-element.272) | copy-start | bytes 3631108
  345.8 16.3 %copy-start.115 = (f32[394]{0:T(512)}, f32[394]{0:T(512)S(1)}, u32[]{:S(2)}) copy-start(f32[394]{0:T(512)S(1)} %broadcast_multiply_fusion.3) | copy-start | bytes 4732
  346.1 16.0 %copy-start.127 = (f32[394]{0:T(512)}, f32[394]{0:T(512)S(1)}, u32[]{:S(2)}) copy-start(f32[394]{0:T(512)S(1)} %multiply_reduce_fusion.19) | copy-start | bytes 4732
  346.2 16.0 %copy-start.121 = (f32[394]{0:T(512)}, f32[394]{0:T(512)S(1)}, u32[]{:S(2)}) copy-start(f32[394]{0:T(512)S(1)} %fusion.117) | copy-start | bytes 4732
  346.4 15.7 %copy-start.53 = (bf16[394,768]{1,0:T(8,128)(2,1)}, bf16[394,768]{1,0:T(8,128)(2,1)S(1)}, u32[]{:S(2)}) copy-start(bf16[394,768]{1,0:T(8,128)(2,1)S(1)} %add_convert_fusion.5) | copy-start | bytes 1815556
  346.5 15.7 %copy-start.142 = (f32[3072]{0:T(1024)}, f32[3072]{0:T(1024)S(1)}, u32[]{:S(2)}) copy-start(f32[3072]{0:T(1024)S(1)} %get-tuple-element.321) | copy-start | bytes 36868
  347.8 14.4 %slice-start.5 = ((s8[4718592]{0:T(1024)(128)(4,1)}), s8[524288]{0:T(1024)(128)(4,1)S(1)}, s32[]{:S(2)}) async-start(s8[4718592]{0:T(1024)(128)(4,1)} %bitcast.397), calls=%async_computation.5 | async-start | bytes 1048576
  365.4 98.9 %copy-start.12 = (f32[394,768]{1,0:T(8,128)}, f32[394,768]{1,0:T(8,128)S(1)}, u32[]{:S(2)}) copy-start(f32[394,768]{1,0:T(8,128)S(1)} %get-tuple-element.268) | copy-start | bytes 3631108
  384.1 11.2 copy-start.19
  431.5 9.2 copy-start.31
  447.7 10.2 copy-start.26
  464.4 18.2 %slice-start.8 = ((s8[4718592]{0:T(1024)(128)(4,1)}), s8[4194304]{0:T(1024)(128)(4,1)S(1)}, s32[]{:S(2)}) async-start(s8[4718592]{0:T(1024)(128)(4,1)} %bitcast.405), calls=%async_computation.8 | async-start | bytes 8388608
  466.2 16.4 %copy-start.8 = (f32[394,768]{1,0:T(8,128)}, f32[394,768]{1,0:T(8,128)S(1)}, u32[]{:S(2)}) copy-start(f32[394,768]{1,0:T(8,128)S(1)} %get-tuple-element.266) | copy-start | bytes 3631108
  466.8 15.8 %copy-start.55 = (bf16[394,768]{1,0:T(8,128)(2,1)}, bf16[394,768]{1,0:T(8,128)(2,1)S(1)}, u32[]{:S(2)}) copy-start(bf16[394,768]{1,0:T(8,128)(2,1)S(1)} %add_convert_fusion.3) | copy-start | bytes 1815556
  466.8 15.8 %copy-start.133 = (f32[768]{0:T(1024)S(1)}, f32[768]{0:T(1024)}, u32[]{:S(2)}) copy-start(f32[768]{0:T(1024)} %get-tuple-element.298) | copy-start | bytes 9220
  466.8 15.8 %copy-start.153 = (f32[768]{0:T(1024)S(1)}, f32[768]{0:T(1024)}, u32[]{:S(2)}) copy-start(f32[768]{0:T(1024)} %get-tuple-element.297) | copy-start | bytes 9220
  466.8 15.8 %slice-start.9 = ((s8[4718592]{0:T(1024)(128)(4,1)}), s8[524288]{0:T(1024)(128)(4,1)S(1)}, s32[]{:S(2)}) async-start(s8[4718592]{0:T(1024)(128)(4,1)} %bitcast.405), calls=%async_computation.9 | async-start | bytes 1048576
  526.1 11.4 %slice-start.6 = ((s8[4718592]{0:T(1024)(128)(4,1)}), s8[4194304]{0:T(1024)(128)(4,1)S(1)}, s32[]{:S(2)}) async-start(s8[4718592]{0:T(1024)(128)(4,1)} %bitcast.401), calls=%async_computation.6 | async-start | bytes 8388608
  528.2 9.2 copy-start.64
  528.2 9.2 copy-start.9
  528.2 9.2 slice-start.7
  595.0 10.1 slice-start.2
  596.1 9.0 copy-start.59
  596.1 9.0 copy-start.7
  596.1 9.0 copy-start.109
  596.1 9.0 copy-start.116
  596.1 9.0 copy-start.122
  719.7 11.7 %copy-start.76 = (s32[14,14]{1,0:T(8,128)S(1)}, s32[14,14]{1,0:T(8,128)}, u32[]{:S(2)}) copy-start(s32[14,14]{1,0:T(8,128)} %copy-done.75) | copy-start | bytes 2356
  832.2 286.6 %copy-start.80 = (f32[42144]{0:T(1024)S(1)}, f32[42144]{0:T(1024)}, u32[]{:S(2)}) copy-start(f32[42144]{0:T(1024)} %param.36) | copy-start | bytes 505732
  832.2 286.6 %copy-start.98 = (f32[42144]{0:T(1024)S(1)}, f32[42144]{0:T(1024)}, u32[]{:S(2)}) copy-start(f32[42144]{0:T(1024)} %param.37) | copy-start | bytes 505732
  832.2 288.5 %copy-start.40 = (f32[2048,96]{0,1:T(8,128)S(1)}, f32[2048,96]{0,1:T(8,128)}, u32[]{:S(2)}) copy-start(f32[2048,96]{0,1:T(8,128)} %param.33) | copy-start | bytes 2359300
  832.2 288.5 %copy-start.83 = (f32[2048,96]{0,1:T(8,128)S(1)}, f32[2048,96]{0,1:T(8,128)}, u32[]{:S(2)}) copy-start(f32[2048,96]{0,1:T(8,128)} %param.34) | copy-start | bytes 2359300
  (132 other events, 465.4 us)

commit v2 on v1

--- a/solution.py
+++ b/solution.py
@@ -22,7 +22,6 @@
 
 
 MESH = pl.DeviceIdType.MESH
-HIGHEST = lax.Precision.HIGHEST
 NORM_EPS = 1e-06
 CLIP_NORM = 0.02
 LEARN_RATE = 0.03
@@ -47,23 +46,6 @@
     return jnp.concatenate(
         [vectors.reshape(-1), fc_bias.reshape(-1), rel_tables.reshape(-1), special.reshape(-1)]
     )
-
-
-def layer_norm(values, gain_vec, shift_vec):
-    average = jnp.mean(values, -1, keepdims=True)
-    centred = values - average
-    variance = jnp.mean(centred * centred, -1, keepdims=True)
-    return centred * lax.rsqrt(variance + NORM_EPS) * gain_vec + shift_vec
-
-
-def softmax_rows(scores):
-    highest = jnp.max(scores, -1, keepdims=True)
-    exponent = jnp.exp(scores - highest)
-    return exponent / jnp.sum(exponent, -1, keepdims=True)
-
-
-def exact_gelu(values):
-    return jax.nn.gelu(values, approximate=False)
 
 
 def adam_update(weight, moment_one, moment_two, gradient, factor, decay_rate):
@@ -78,47 +60,554 @@
     return (weight - LEARN_RATE * (direction + decay_rate * weight), new_first, new_second)
 
 
-def offset_table():
+IMG = 208
+TILE = 128
+REL_LANES = 768
+KEY_LANES = 384
+
+
+def dot_nn(x, w):
+    return lax.dot_general(x, w, (((1,), (0,)), ((), ())), preferred_element_type=jnp.float32)
+
+
+def dot_nt(x, w):
+    return lax.dot_general(x, w, (((1,), (1,)), ((), ())), preferred_element_type=jnp.float32)
+
+
+def dot_tn(x, w):
+    return lax.dot_general(x, w, (((0,), (0,)), ((), ())), preferred_element_type=jnp.float32)
+
+
+def three_parts(values):
+    high = values.astype(jnp.bfloat16)
+    rest = values - high.astype(jnp.float32)
+    middle = rest.astype(jnp.bfloat16)
+    low = (rest - middle.astype(jnp.float32)).astype(jnp.bfloat16)
+    return high, middle, low
+
+
+def exact_nn(values, hot):
+    return sum(dot_nn(part, hot) for part in three_parts(values))
+
+
+def exact_left(hot, values):
+    return sum(dot_nn(hot, part) for part in three_parts(values))
+
+
+def col_sum(values):
+    return jnp.sum(values, 0, keepdims=True)
+
+
+def norm_parts(values):
+    average = jnp.mean(values, -1, keepdims=True)
+    centred = values - average
+    variance = jnp.mean(centred * centred, -1, keepdims=True)
+    scale = lax.rsqrt(variance + NORM_EPS)
+    return centred * scale, scale
+
+
+def norm_backward(upstream, values, gain):
+    unit, scale = norm_parts(values)
+    d_gain = col_sum(upstream * unit)
+    d_shift = col_sum(upstream)
+    d_unit = upstream * gain
+    mean_one = jnp.mean(d_unit, -1, keepdims=True)
+    mean_two = jnp.mean(d_unit * unit, -1, keepdims=True)
+    return scale * (d_unit - mean_one - unit * mean_two), d_gain, d_shift
+
+
+def iota(shape, axis):
+    return lax.broadcasted_iota(jnp.int32, shape, axis)
+
+
+def bias_kernel(rel_ref, extra_ref, out_ref, wide_ref):
     extent = 2 * GRID - 1
-    place = jnp.arange(GRID)
-    return (
-        place[:, None, None] - place[None, :, None] + GRID - 1 == jnp.arange(extent)[None, None, :]
-    ).astype(jnp.float32)
-
-
-def bias_block(rel_local, axis_hot):
-    heads_here = rel_local.shape[0]
+    line = jnp.broadcast_to(rel_ref[0], (16, REL_LANES))
+    line = pltpu.roll(line, 0, 1, stride=1, stride_axis=0)
+    for p in range(GRID):
+        first = (GRID - 1 - p) * extent + GRID - 1
+        turned = pltpu.roll(line, REL_LANES - first, 1)
+        wide_ref[pl.ds(16 * p, 16), :] = turned[:, :KEY_LANES]
+    lane = iota((KEY_LANES, IMG), 0)
+    key = iota((KEY_LANES, IMG), 1) - 1
+    place = lax.div(key, GRID) * extent + lax.rem(key, GRID)
+    columns = ((lane == place) & (key >= 0) & (key < PATCH)).astype(jnp.bfloat16)
+    row = iota((IMG, 16 * GRID), 0) - 1
+    spot = iota((IMG, 16 * GRID), 1)
+    place = lax.div(row, GRID) * 16 + lax.rem(row, GRID)
+    rows = ((spot == place) & (row >= 0) & (row < PATCH)).astype(jnp.bfloat16)
+    inner = exact_left(rows, exact_nn(wide_ref[...], columns))
+    query = iota((IMG, IMG), 0)
+    key = iota((IMG, IMG), 1)
+    extra = extra_ref[0]
+    inner = jnp.where(query == 0, extra[:, 0:1], inner)
+    inner = jnp.where(key == 0, jnp.where(query == 0, extra[:, 2:3], extra[:, 1:2]), inner)
+    out_ref[0] = jnp.where(key < SEQ, inner, -1e30)
+
+
+def rel_biases(rel_tables):
+    number = LAYERS * H
+    flat = rel_tables.reshape(number, 1, NREL)
+    reverse = jnp.pad(flat[:, :, NREL - 4 :: -1], ((0, 0), (0, 0), (0, REL_LANES - NREL + 3)))
+    extras = jnp.pad(flat[:, :, NREL - 3 :], ((0, 0), (0, 0), (0, TILE - 3)))
+    return pl.pallas_call(
+        bias_kernel,
+        grid=(number,),
+        in_specs=[
+            pl.BlockSpec((1, 1, REL_LANES), lambda i: (i, 0, 0)),
+            pl.BlockSpec((1, 1, TILE), lambda i: (i, 0, 0)),
+        ],
+        out_specs=pl.BlockSpec((1, IMG, IMG), lambda i: (i, 0, 0)),
+        out_shape=jax.ShapeDtypeStruct((number, IMG, IMG), jnp.float32),
+        scratch_shapes=[pltpu.VMEM((16 * GRID, KEY_LANES), jnp.float32)],
+        name="rel_biases",
+    )(reverse, extras)
+
+
+def rel_grad_kernel(sums_ref, rel_ref, extra_ref):
     extent = 2 * GRID - 1
-    inner = rel_local[:, : extent * extent].reshape(heads_here, extent, extent)
-    across = jnp.einsum("hij,qsj->hiqs", inner, axis_hot, precision=HIGHEST)
-    spread = jnp.einsum("hiqs,pri->hpqrs", across, axis_hot, precision=HIGHEST).reshape(
-        heads_here, PATCH, PATCH
+    sums = sums_ref[0]
+    column = iota((IMG, KEY_LANES), 0) - 1
+    lane = iota((IMG, KEY_LANES), 1)
+    place = lax.div(column, GRID) * extent + lax.rem(column, GRID)
+    columns = ((lane == place) & (column >= 0) & (column < PATCH)).astype(jnp.bfloat16)
+    spot = iota((16 * GRID, IMG), 0)
+    row = iota((16 * GRID, IMG), 1) - 1
+    place = lax.div(row, GRID) * 16 + GRID - 1 - lax.rem(row, GRID)
+    rows = ((spot == place) & (row >= 0) & (row < PATCH)).astype(jnp.bfloat16)
+    wide = exact_nn(exact_left(rows, sums), columns)
+    wide = jnp.concatenate([wide, jnp.zeros((16 * GRID, REL_LANES - KEY_LANES), jnp.float32)], 1)
+    total = jnp.zeros((16, REL_LANES), jnp.float32)
+    for p in range(GRID):
+        first = (GRID - 1 - p) * extent
+        total += pltpu.roll(wide[16 * p : 16 * p + 16], first, 1) if first else wide[16 * p : 16 * p + 16]
+    rel_ref[0] = col_sum(pltpu.roll(total, 0, 1, stride=1, stride_axis=0))
+    query = iota((IMG, IMG), 0)
+    key = iota((IMG, IMG), 1)
+    lanes = iota((1, TILE), 1)
+    result = jnp.zeros((1, TILE), jnp.float32)
+    for k, mask in enumerate(
+        ((query == 0) & (key > 0), (query > 0) & (key == 0), (query == 0) & (key == 0))
+    ):
+        amount = jnp.sum(col_sum(jnp.where(mask, sums, 0.0)), 1, keepdims=True)
+        result = jnp.where(lanes == k, amount, result)
+    extra_ref[0] = result
+
+
+def rel_grads(score_sums):
+    number = LAYERS * H
+    rel, extra = pl.pallas_call(
+        rel_grad_kernel,
+        grid=(number,),
+        in_specs=[pl.BlockSpec((1, IMG, IMG), lambda i: (i, 0, 0))],
+        out_specs=[
+            pl.BlockSpec((1, 1, REL_LANES), lambda i: (i, 0, 0)),
+            pl.BlockSpec((1, 1, TILE), lambda i: (i, 0, 0)),
+        ],
+        out_shape=[
+            jax.ShapeDtypeStruct((number, 1, REL_LANES), jnp.float32),
+            jax.ShapeDtypeStruct((number, 1, TILE), jnp.float32),
+        ],
+        name="rel_grads",
+    )(score_sums)
+    inner = rel[:, 0, NREL - 4 :: -1]
+    return jnp.concatenate([inner, extra[:, 0, :3]], 1).reshape(LAYERS, H, NREL)
+
+
+def head_views(k):
+    return ((0, 1, 2, 1, 0, 0), (0, 1, 2, 1, 1, 1), (3, 4, 3, 0, 0, 1))[k]
+
+
+def half_mask(rows, half):
+    return (iota((rows, TILE), 1) < TILE // 2) == (half == 0)
+
+
+def keep_half(values, half):
+    return jnp.where(half_mask(values.shape[0], half), values, jnp.zeros_like(values))
+
+
+def tile_of(ref, member, image, tile):
+    return ref[member, pl.ds(image * IMG, IMG), pl.ds(tile * TILE, TILE)]
+
+
+def head_probs(proj_ref, rel_ref, member, image, k):
+    qt, kt, vt, ot, qk_half, vo_half = head_views(k)
+    query = keep_half(tile_of(proj_ref, member, image, qt), qk_half)
+    key = tile_of(proj_ref, member, image, kt)
+    scores = dot_nt(query, key) * (DH ** (-0.5)) + rel_ref[3 * member + k]
+    exponent = jnp.exp(scores - jnp.max(scores, -1, keepdims=True))
+    return exponent / jnp.sum(exponent, -1, keepdims=True), query, key
+
+
+def member_cols(member, first, width):
+    return pl.ds(pl.multiple_of(member * (6 * TILE) + first * TILE, TILE), width * TILE)
+
+
+def loop(number, body):
+    def step(i, unused):
+        body(i)
+        return 0
+
+    lax.fori_loop(0, number, step, 0)
+
+
+def load(src, dst, sem):
+    copy = pltpu.make_async_copy(src, dst, sem)
+    copy.start()
+    return copy
+
+
+def embed_kernel(members, images, codes_ref, kind_ref, special_ref, table_hbm, x_ref, table_buf, sems):
+    chunk = table_buf.shape[2]
+    number = table_hbm.shape[1] // chunk
+    for j in range(2):
+        load(table_hbm.at[:, pl.ds(j * chunk, chunk)], table_buf.at[j], sems.at[j])
+    x_ref[...] = jnp.zeros_like(x_ref)
+
+    def body(j):
+        slot = lax.rem(j, 2)
+        src = table_hbm.at[:, pl.ds(pl.multiple_of(j * chunk, TILE), chunk)]
+        pltpu.make_async_copy(src, table_buf.at[slot], sems.at[slot]).wait()
+        hot = (codes_ref[...] == iota((codes_ref.shape[0], chunk), 1) + j * chunk).astype(
+            jnp.bfloat16
+        )
+        x_ref[...] += dot_nt(hot, table_buf[slot])
+
+        @pl.when(j + 2 < number)
+        def _():
+            src = table_hbm.at[:, pl.ds(pl.multiple_of((j + 2) * chunk, TILE), chunk)]
+            load(src, table_buf.at[slot], sems.at[slot])
+
+    loop(number, body)
+    kind = kind_ref[...]
+    fallback = jnp.where(kind == 1, special_ref[0:1, :], special_ref[1:2, :])
+    x_ref[...] = jnp.where(kind == 0, x_ref[...], fallback)
+
+
+def forward_kernel(
+    members, images, x_ref, vec_ref, fc_ref, proj_bias_ref, rel_ref, attn_hbm, up_hbm, down_hbm,
+    next_ref, proj_ref, mixed_ref, attn_out_ref, mid_ref, mlp_in_ref, pre_ref, act_ref, mlp_ref,
+    attn_buf, up_buf, down_buf, sems,
+):
+    copies = [
+        load(src, dst, sems.at[i])
+        for i, (src, dst) in enumerate(
+            ((attn_hbm, attn_buf), (up_hbm, up_buf), (down_hbm, down_buf))
+        )
+    ]
+    unit, unused = norm_parts(x_ref[...])
+    attn_in = (unit * vec_ref[0:1, :] + vec_ref[1:2, :]).astype(jnp.bfloat16)
+    copies[0].wait()
+    attn_out_ref[...] = jnp.broadcast_to(vec_ref[4:5, :], attn_out_ref.shape)
+
+    def body(m):
+        cols = member_cols(m, 0, 5)
+        proj_ref[m] = (dot_nn(attn_in, attn_buf[:, cols]) + proj_bias_ref[:, cols]).astype(
+            jnp.bfloat16
+        )
+        for image in range(images):
+            outs = []
+            for k in range(3):
+                probs, unused, unused = head_probs(proj_ref, rel_ref, m, image, k)
+                value = tile_of(proj_ref, m, image, head_views(k)[2])
+                outs.append(dot_nn(probs.astype(jnp.bfloat16), value))
+            rows = pl.ds(image * IMG, IMG)
+            mixed_ref[m, rows, pl.ds(0, TILE)] = keep_half(outs[2], 1).astype(jnp.bfloat16)
+            mixed_ref[m, rows, pl.ds(TILE, TILE)] = jnp.where(
+                half_mask(IMG, 0), outs[0], outs[1]
+            ).astype(jnp.bfloat16)
+        attn_out_ref[...] += dot_nt(mixed_ref[m], attn_buf[:, member_cols(m, 4, 2)])
+
+    loop(members, body)
+    mid = x_ref[...] + vec_ref[5:6, :] * attn_out_ref[...]
+    mid_ref[...] = mid
+    unit, unused = norm_parts(mid)
+    mlp_in_ref[...] = (unit * vec_ref[6:7, :] + vec_ref[7:8, :]).astype(jnp.bfloat16)
+    copies[1].wait()
+    copies[2].wait()
+    mlp_ref[...] = jnp.broadcast_to(vec_ref[8:9, :], mlp_ref.shape)
+
+    def feed(j):
+        cols = pl.ds(pl.multiple_of(j * D, TILE), D)
+        pre = dot_nn(mlp_in_ref[...], up_buf[:, cols]) + fc_ref[:, cols]
+        pre_ref[:, cols] = pre
+        act = (0.5 * pre * (1.0 + lax.erf(pre * (0.5**0.5)))).astype(jnp.bfloat16)
+        act_ref[:, cols] = act
+        mlp_ref[...] += dot_nt(act, down_buf[:, cols])
+
+    loop(FF // D, feed)
+    next_ref[...] = mid_ref[...] + vec_ref[9:10, :] * mlp_ref[...]
+
+
+def head_kernel(
+    images, slots, x_ref, special_ref, spots_ref, targets_ref, weight_ref, valid_ref, table_hbm,
+    loss_ref, up_ref, gain_ref, shift_ref, picked_ref, picked_t_ref, d_logits_ref,
+    table_buf, logits_ref, dpick_ref, sems,
+):
+    chunk = 1024
+    number = table_hbm.shape[1] // chunk
+    per = slots // images
+    copies = [
+        load(
+            table_hbm.at[:, pl.ds(j * chunk, chunk)],
+            table_buf.at[:, pl.ds(j * chunk, chunk)],
+            sems.at[j],
+        )
+        for j in range(number)
+    ]
+    unit, unused = norm_parts(x_ref[...])
+    normed = (unit * special_ref[2:3, :] + special_ref[3:4, :]).astype(jnp.bfloat16)
+    hots = []
+    for image in range(images):
+        spots = spots_ref[pl.ds(image * per, per), :]
+        hots.append((spots == iota((per, IMG), 1)).astype(jnp.bfloat16))
+        picked_ref[pl.ds(image * per, per), :] = dot_nn(
+            hots[image], normed[image * IMG : (image + 1) * IMG]
+        ).astype(jnp.bfloat16)
+    picked = picked_ref[...]
+    high = jnp.full((slots, 1), -1e30, jnp.float32)
+    for j in range(number):
+        cols = pl.ds(j * chunk, chunk)
+        copies[j].wait()
+        part = dot_nn(picked, table_buf[:, cols])
+        logits_ref[:, cols] = part
+        high = jnp.maximum(high, jnp.max(part, 1, keepdims=True))
+    total = jnp.zeros((slots, 1), jnp.float32)
+    target = jnp.zeros((slots, 1), jnp.float32)
+    for j in range(number):
+        part = logits_ref[:, pl.ds(j * chunk, chunk)]
+        total += jnp.sum(jnp.exp(part - high), 1, keepdims=True)
+        hit = targets_ref[...] == iota((slots, chunk), 1) + j * chunk
+        target += jnp.sum(jnp.where(hit, part, 0.0), 1, keepdims=True)
+    log_total = high + jnp.log(total)
+    loss_ref[...] = jnp.broadcast_to(
+        col_sum((log_total - target) * valid_ref[...]), loss_ref.shape
     )
-    top_row = jnp.concatenate(
-        [
-            rel_local[:, NREL - 1][:, None, None],
-            jnp.broadcast_to(rel_local[:, NREL - 3][:, None, None], (heads_here, 1, PATCH)),
+    dpick_ref[...] = jnp.zeros_like(dpick_ref)
+    for j in range(number):
+        cols = pl.ds(j * chunk, chunk)
+        hit = targets_ref[...] == iota((slots, chunk), 1) + j * chunk
+        d_part = (
+            (jnp.exp(logits_ref[:, cols] - log_total) - jnp.where(hit, 1.0, 0.0)) * weight_ref[...]
+        ).astype(jnp.bfloat16)
+        d_logits_ref[:, cols] = d_part
+        dpick_ref[...] += dot_nt(d_part, table_buf[:, cols])
+    normed_grads = []
+    for image in range(images):
+        d_part = dpick_ref[pl.ds(image * per, per), :]
+        normed_grads.append(sum(dot_tn(hots[image], part) for part in three_parts(d_part)))
+    upstream, gain, shift = norm_backward(
+        jnp.concatenate(normed_grads, 0), x_ref[...], special_ref[2:3, :]
+    )
+    up_ref[...] = upstream
+    gain_ref[...] = gain
+    shift_ref[...] = shift
+    picked_t_ref[...] = picked.T
+
+
+def backward_kernel(
+    members, images, up_ref, x_ref, vec_ref, rel_ref, proj_ref, mixed_ref, attn_out_ref, mid_ref,
+    mlp_in_ref, mlp_ref, pre_hbm, attn_hbm, up_hbm, down_hbm,
+    next_ref, vec_grad_ref, fc_grad_ref, proj_grad_ref, sums_ref, d_pre_ref, d_cat_ref,
+    attn_in_t_ref, g_attn_t_ref, mlp_in_t_ref, g_mlp_t_ref,
+    attn_buf, up_buf, down_buf, pre_buf, acc_ref, mid_grad_ref, sems,
+):
+    copies = [
+        load(src, dst, sems.at[i])
+        for i, (src, dst) in enumerate(
+            ((down_hbm, down_buf), (pre_hbm, pre_buf), (up_hbm, up_buf), (attn_hbm, attn_buf))
+        )
+    ]
+    bf = jnp.bfloat16
+    upstream = up_ref[...]
+    g_mlp = (vec_ref[9:10, :] * upstream).astype(bf)
+    g_mlp_t_ref[...] = g_mlp.T
+    vec_grad_ref[9:10, :] = col_sum(upstream * mlp_ref[...])
+    vec_grad_ref[8:9, :] = col_sum(g_mlp.astype(jnp.float32))
+    mlp_in_t_ref[...] = mlp_in_ref[...].T
+    acc_ref[...] = jnp.zeros_like(acc_ref)
+    for copy in copies[:3]:
+        copy.wait()
+
+    def feed(j):
+        cols = pl.ds(pl.multiple_of(j * D, TILE), D)
+        pre = pre_buf[:, cols]
+        slope = 0.5 * (1.0 + lax.erf(pre * (0.5**0.5))) + pre * jnp.exp(-0.5 * pre * pre) * (
+            (2.0 * jnp.pi) ** (-0.5)
+        )
+        d_pre = (dot_nn(g_mlp, down_buf[:, cols]) * slope).astype(bf)
+        d_pre_ref[:, cols] = d_pre
+        fc_grad_ref[:, cols] = col_sum(d_pre.astype(jnp.float32))
+        acc_ref[...] += dot_nt(d_pre, up_buf[:, cols])
+
+    loop(FF // D, feed)
+    d_mid, gain, shift = norm_backward(acc_ref[...], mid_ref[...], vec_ref[6:7, :])
+    vec_grad_ref[6:7, :] = gain
+    vec_grad_ref[7:8, :] = shift
+    d_mid = d_mid + up_ref[...]
+    mid_grad_ref[...] = d_mid
+    g_attn = (vec_ref[5:6, :] * d_mid).astype(bf)
+    g_attn_t_ref[...] = g_attn.T
+    vec_grad_ref[5:6, :] = col_sum(d_mid * attn_out_ref[...])
+    vec_grad_ref[4:5, :] = col_sum(g_attn.astype(jnp.float32))
+    acc_ref[...] = jnp.zeros_like(acc_ref)
+    copies[3].wait()
+
+    def body(m):
+        d_mixed = dot_nn(g_attn, attn_buf[:, member_cols(m, 4, 2)]).astype(bf)
+        for image in range(images):
+            rows = pl.ds(image * IMG, IMG)
+            d_value, d_query, d_key = [], [], []
+            for k in range(3):
+                qt, kt, vt, ot, qk_half, vo_half = head_views(k)
+                probs, query, key = head_probs(proj_ref, rel_ref, m, image, k)
+                value = tile_of(proj_ref, m, image, vt)
+                d_out = keep_half(
+                    d_mixed[image * IMG : (image + 1) * IMG, ot * TILE : (ot + 1) * TILE], vo_half
+                )
+                d_value.append(dot_tn(probs.astype(bf), d_out))
+                d_probs = dot_nt(d_out, value)
+                d_scores = (
+                    probs * (d_probs - jnp.sum(probs * d_probs, -1, keepdims=True))
+                ).astype(bf)
+                if image:
+                    sums_ref[3 * m + k] += d_scores.astype(jnp.float32)
+                else:
+                    sums_ref[3 * m + k] = d_scores.astype(jnp.float32)
+                d_query.append(dot_nn(d_scores, keep_half(key, qk_half)) * (DH ** (-0.5)))
+                d_key.append(dot_tn(d_scores, query) * (DH ** (-0.5)))
+            tiles = (
+                d_query[0] + d_query[1],
+                d_key[0] + d_key[1],
+                d_value[0] + d_value[1],
+                d_query[2] + d_value[2],
+                d_key[2],
+                jnp.zeros((IMG, TILE), jnp.float32),
+            )
+            for t, tile in enumerate(tiles):
+                d_cat_ref[m, rows, pl.ds(t * TILE, TILE)] = tile.astype(bf)
+        d_cat = d_cat_ref[m]
+        proj_grad_ref[:, member_cols(m, 0, 6)] = col_sum(d_cat.astype(jnp.float32))
+        acc_ref[...] += dot_nt(d_cat[:, : 5 * TILE], attn_buf[:, member_cols(m, 0, 5)])
+
+    loop(members, body)
+    d_input, gain, shift = norm_backward(acc_ref[...], x_ref[...], vec_ref[0:1, :])
+    vec_grad_ref[0:1, :] = gain
+    vec_grad_ref[1:2, :] = shift
+    vec_grad_ref[2:4, :] = jnp.zeros((2, D), jnp.float32)
+    next_ref[...] = d_input + mid_grad_ref[...]
+    unit, unused = norm_parts(x_ref[...])
+    attn_in = (unit * vec_ref[0:1, :] + vec_ref[1:2, :]).astype(bf)
+    attn_in_t_ref[...] = attn_in.T
+
+
+VMEM_SPEC = pl.BlockSpec(memory_space=pltpu.VMEM)
+ANY_SPEC = pl.BlockSpec(memory_space=pl.ANY)
+COMPUTE_PARAMS = pltpu.CompilerParams(vmem_limit_bytes=60 * 2**20)
+
+
+def shaped(shape, kind=jnp.float32):
+    return jax.ShapeDtypeStruct(shape, kind)
+
+
+def embed(codes, kind, special, table, members, images):
+    rows = images * IMG
+    chunk = 1024
+    return pl.pallas_call(
+        functools.partial(embed_kernel, members, images),
+        out_shape=shaped((rows, D)),
+        in_specs=[VMEM_SPEC] * 3 + [ANY_SPEC],
+        out_specs=VMEM_SPEC,
+        scratch_shapes=[pltpu.VMEM((2, D, chunk), jnp.bfloat16), pltpu.SemaphoreType.DMA((2,))],
+        compiler_params=COMPUTE_PARAMS,
+        name="embed",
+    )(codes, kind, special, table)
+
+
+def forward_layer(x, vec, fc, proj_bias, rel, mats, members, images):
+    rows = images * IMG
+    bf = jnp.bfloat16
+    return pl.pallas_call(
+        functools.partial(forward_kernel, members, images),
+        out_shape=[
+            shaped((rows, D)),
+            shaped((members, rows, 5 * TILE), bf),
+            shaped((members, rows, 2 * TILE), bf),
+            shaped((rows, D)),
+            shaped((rows, D)),
+            shaped((rows, D), bf),
+            shaped((rows, FF)),
+            shaped((rows, FF), bf),
+            shaped((rows, D)),
         ],
-        2,
-    )
-    lower_rows = jnp.concatenate(
-        [jnp.broadcast_to(rel_local[:, NREL - 2][:, None, None], (heads_here, PATCH, 1)), spread], 2
-    )
-    return jnp.concatenate([top_row, lower_rows], 1)
-
-
-def bias_grad(score_sums, axis_hot):
-    heads_here = score_sums.shape[0]
-    extent = 2 * GRID - 1
-    inner = score_sums[:, 1:, 1:].reshape(heads_here, GRID, GRID, GRID, GRID)
-    across = jnp.einsum("hpqrs,qsj->hprj", inner, axis_hot, precision=HIGHEST)
-    folded = jnp.einsum("hprj,pri->hij", across, axis_hot, precision=HIGHEST).reshape(
-        heads_here, extent * extent
-    )
-    extras = jnp.stack(
-        [jnp.sum(score_sums[:, 0, 1:], 1), jnp.sum(score_sums[:, 1:, 0], 1), score_sums[:, 0, 0]], 1
-    )
-    return jnp.concatenate([folded, extras], 1)
+        in_specs=[VMEM_SPEC] * 5 + [ANY_SPEC] * 3,
+        out_specs=[VMEM_SPEC] * 9,
+        scratch_shapes=[pltpu.VMEM((D, 4 * D), bf)] * 3 + [pltpu.SemaphoreType.DMA((3,))],
+        compiler_params=COMPUTE_PARAMS,
+        name="forward_layer",
+    )(x, vec, fc, proj_bias, rel, *mats)
+
+
+def head_and_loss(x, special, spots, targets, weight, valid, table, images):
+    rows = images * IMG
+    slots = spots.shape[0]
+    bf = jnp.bfloat16
+    return pl.pallas_call(
+        functools.partial(head_kernel, images, slots),
+        out_shape=[
+            shaped((8, TILE)),
+            shaped((rows, D)),
+            shaped((1, D)),
+            shaped((1, D)),
+            shaped((slots, D), bf),
+            shaped((D, slots), bf),
+            shaped((slots, V), bf),
+        ],
+        in_specs=[VMEM_SPEC] * 6 + [ANY_SPEC],
+        out_specs=[VMEM_SPEC] * 7,
+        scratch_shapes=[
+            pltpu.VMEM((D, V), bf),
+            pltpu.VMEM((slots, V), jnp.float32),
+            pltpu.VMEM((slots, D), jnp.float32),
+            pltpu.SemaphoreType.DMA((V // 1024,)),
+        ],
+        compiler_params=COMPUTE_PARAMS,
+        name="head_and_loss",
+    )(x, special, spots, targets, weight, valid, table)
+
+
+def backward_layer(upstream, x, vec, rel, kept, mats, members, images):
+    rows = images * IMG
+    bf = jnp.bfloat16
+    proj, mixed, attn_out, mid, mlp_in, pre, mlp = kept
+    attn_mat, up_mat, down_mat = mats
+    return pl.pallas_call(
+        functools.partial(backward_kernel, members, images),
+        out_shape=[
+            shaped((rows, D)),
+            shaped((10, D)),
+            shaped((1, FF)),
+            shaped((1, 4 * D)),
+            shaped((H, IMG, IMG)),
+            shaped((rows, FF), bf),
+            shaped((members, rows, 6 * TILE), bf),
+            shaped((D, rows), bf),
+            shaped((D, rows), bf),
+            shaped((D, rows), bf),
+            shaped((D, rows), bf),
+        ],
+        in_specs=[VMEM_SPEC] * 10 + [ANY_SPEC] * 4,
+        out_specs=[VMEM_SPEC] * 11,
+        scratch_shapes=[pltpu.VMEM((D, 4 * D), bf)] * 3
+        + [
+            pltpu.VMEM((rows, FF), jnp.float32),
+            pltpu.VMEM((rows, D), jnp.float32),
+            pltpu.VMEM((rows, D), jnp.float32),
+            pltpu.SemaphoreType.DMA((4,)),
+        ],
+        compiler_params=COMPUTE_PARAMS,
+        name="backward_layer",
+    )(upstream, x, vec, rel, proj, mixed, attn_out, mid, mlp_in, mlp, pre, attn_mat, up_mat, down_mat)
 
 
 def factor(ndp):
@@ -320,7 +809,8 @@
                 copy.wait_send()
 
 
-def reduce_kernel(outer, inner, members, rows, halves, groups, arrays, lags, *refs):
+def reduce_kernel(outer, inner, members, rows, halves, groups, counts, lags, *refs):
+    left_count, right_count, arrays = counts
     refs = list(refs)
 
     def take(number):
@@ -328,12 +818,13 @@
         del refs[:number]
         return taken
 
-    (small_in,) = take(1)
-    lefts = take(arrays)
-    rights = take(arrays)
+    small_in, codes = take(2)
+    lefts = take(left_count)
+    rights = take(right_count)
     outs = take(arrays)
     small_out, square_out = take(2)
-    right_buf, right_sem = take(2)
+    right_bufs = take(2)
+    (right_sem,) = take(1)
     sent0, got0, own0 = take(3)
     sent1a, got1a, keep1a, sent1b, got1b, keep1b = take(6)
     sent2a, got2a, sent2b, got2b, keep2 = take(5)
@@ -367,29 +858,46 @@
         lax.fori_loop(0, members, step, 0)
 
     def fetch(turn):
-        i, first, width = groups[turn]
-        block = rights[i].shape[1] // members
-        depth = rights[i].shape[0]
-        return [
-            pltpu.make_async_copy(
-                rights[i].at[:, pl.ds(k * block + first, width)],
-                right_buf.at[turn % 2, k, pl.ds(0, depth), pl.ds(0, width)],
-                right_sem.at[turn % 2, k],
-            )
-            for k in range(members)
-        ]
+        width = groups[turn][2]
+        copies = []
+        for j, (left, right, first, block) in enumerate(groups[turn][3]):
+            if right is None:
+                continue
+            ref = rights[right]
+            depth = ref.shape[-2]
+            for k in range(members):
+                if len(ref.shape) == 3:
+                    src = ref.at[k, :, pl.ds(first, width)]
+                else:
+                    src = ref.at[:, pl.ds(k * block + first, width)]
+                copies.append(
+                    pltpu.make_async_copy(
+                        src,
+                        right_bufs[j].at[turn % 2, k, pl.ds(0, depth), pl.ds(0, width)],
+                        right_sem.at[turn % 2, j, k],
+                    )
+                )
+        return copies
 
     def product(turn, half, k):
-        i, first, width = groups[turn]
-        depth = rights[i].shape[0]
-        return jnp.dot(
-            lefts[i][half],
-            right_buf[turn % 2, k, pl.ds(0, depth), pl.ds(0, width)],
-            preferred_element_type=jnp.float32,
-        ).reshape(outer, inner, rows, width)
+        width = groups[turn][2]
+        total = None
+        for j, (left, right, first, block) in enumerate(groups[turn][3]):
+            ref = lefts[left]
+            x = ref[:, half].reshape(outer * inner * rows, ref.shape[-1])
+            if right is None:
+                spot = lax.broadcasted_iota(jnp.int32, (codes.shape[0], width), 1) + (
+                    k * block + first
+                )
+                y = (codes[...] == spot).astype(jnp.bfloat16)
+            else:
+                y = right_bufs[j][turn % 2, k, pl.ds(0, rights[right].shape[-2]), pl.ds(0, width)]
+            part = jnp.dot(x, y, preferred_element_type=jnp.float32)
+            total = part if total is None else total + part
+        return total.reshape(outer, inner, rows, width)
 
     def make(turn):
-        i, first, width = groups[turn]
+        i, first, width = groups[turn][:3]
         cols = pl.ds(0, width)
         slot = turn % 2
         for copy in fetch(turn):
@@ -413,7 +921,7 @@
         each_member(fill_own)
 
     def stage_one(turn):
-        i, first, width = groups[turn]
+        i, first, width = groups[turn][:3]
         cols = pl.ds(0, width)
         old, new = turn % 2, turn % slots[1]
         upper, lower = pl.ds(0, top), pl.ds(top, low_rows)
@@ -462,7 +970,7 @@
             )
 
     def stage_two(turn):
-        i, first, width = groups[turn]
+        i, first, width = groups[turn][:3]
         cols = pl.ds(0, width)
         old, new = turn % slots[1], turn % slots[2]
         chan2a.before_fill(turn)
@@ -514,7 +1022,7 @@
             )
 
     def stage_three(turn):
-        i, first, width = groups[turn]
+        i, first, width = groups[turn][:3]
         cols = pl.ds(0, width)
         old, new = turn % slots[2], turn % slots[3]
         chan3.before_fill(turn)
@@ -546,7 +1054,7 @@
         )
 
     def stage_four(turn):
-        i, first, width = groups[turn]
+        i, first, width = groups[turn][:3]
         cols = pl.ds(0, width)
         old = turn % slots[3]
         chan3.receive(turn)
@@ -635,37 +1143,42 @@
     return total
 
 
-def reduce_products(pairs, small, ndp, members):
+def reduce_products(lefts, rights, codes, arrays, small, ndp, members):
     outer, inner = factor(ndp)
-    per_device = pairs[0][0].shape[1] // ndp
+    per_device = D // ndp
     rows = -(-per_device // 16) * 16
-    both = outer * inner
-    wide = both * rows <= 400
     halves = (rows // 2, rows // 2) if rows % 32 == 0 else (rows, 0)
     top, low_rows = halves
     low_shape = max(low_rows, 16)
     lags = (1, 3, 5, 7)
     slots = (2, 2, 2, 2)
-    lefts, rights, groups, outs = [], [], [], []
-    for i, (x, y) in enumerate(pairs):
-        depth = x.shape[0]
-        turned = x.T.reshape(both, 2, per_device, depth)
-        turned = jnp.pad(turned, ((0, 0), (0, 0), (0, rows - per_device), (0, 0)))
-        lefts.append(turned.transpose(1, 0, 2, 3).reshape(2, both * rows, depth))
-        rights.append(y)
-        block = y.shape[1] // members
-        width = (512 if block % 512 == 0 else 384) if wide else 256
-        groups += [(i, first, width) for first in range(0, block, width)]
+    spread_lefts = []
+    for x in lefts:
+        x = x.reshape(outer * inner, 2, per_device, x.shape[1])
+        spread_lefts.append(jnp.pad(x, ((0, 0), (0, 0), (0, rows - per_device), (0, 0))))
+    groups, outs = [], []
+    for i, (block, cuts) in enumerate(arrays):
         outs.append(jax.ShapeDtypeStruct((rows, block), jnp.float32))
-    most = max(width for _, _, width in groups)
-    deepest = max(y.shape[0] for y in rights)
-    count = len(pairs)
+        groups += [(i,) + cut for cut in cuts]
+    most = max(group[2] for group in groups)
+    deepest, seconds = 16, (16, TILE)
+    for group in groups:
+        for j, part in enumerate(group[3]):
+            if part[1] is None:
+                continue
+            depth = rights[part[1]].shape[-2]
+            if j:
+                seconds = (max(seconds[0], depth), max(seconds[1], group[2]))
+            else:
+                deepest = max(deepest, depth)
+    counts = (len(lefts), len(rights), len(arrays))
     small_shape = small.shape
     bf, f4 = jnp.bfloat16, jnp.float32
     mem = pltpu.VMEM
     scratch = [
         mem((2, members, deepest, most), bf),
-        pltpu.SemaphoreType.DMA((2, members)),
+        mem((2, members) + seconds, bf),
+        pltpu.SemaphoreType.DMA((2, 2, members)),
         mem((slots[0], members, outer, inner, rows, most), bf),
         mem((slots[0], members, outer, inner, rows, most), bf),
         mem((2, members, outer, inner, rows, most), f4),
@@ -697,19 +1210,19 @@
     vmem = pl.BlockSpec(memory_space=pltpu.VMEM)
     results = pl.pallas_call(
         functools.partial(
-            reduce_kernel, outer, inner, members, rows, halves, groups, count, lags
+            reduce_kernel, outer, inner, members, rows, halves, groups, counts, lags
         ),
         out_shape=outs
         + [jax.ShapeDtypeStruct(small_shape, f4), jax.ShapeDtypeStruct((8, 128), f4)],
-        in_specs=[vmem] * (1 + count) + [pl.BlockSpec(memory_space=pl.ANY)] * count,
-        out_specs=[vmem] * (count + 2),
+        in_specs=[vmem] * (2 + counts[0]) + [pl.BlockSpec(memory_space=pl.ANY)] * counts[1],
+        out_specs=[vmem] * (counts[2] + 2),
         scratch_shapes=scratch,
         compiler_params=pltpu.CompilerParams(
             collective_id=1, has_side_effects=True, vmem_limit_bytes=62 * 2**20
         ),
         name="reduce_products",
-    )(small, *lefts, *rights)
-    return [block[:per_device] for block in results[:count]], results[count], results[count + 1]
+    )(small, codes, *spread_lefts, *rights)
+    return [block[:per_device] for block in results[:-2]], results[-2], results[-1]
 
 
 def local(members, ndp, *args):
@@ -725,20 +1238,19 @@
     bf, f4 = jnp.bfloat16, jnp.float32
     member = lax.axis_index("mp")
     images = patch_codes.shape[0] // members
-    rows_all = images * SEQ
-    depth = -(-rows_all // 16) * 16
-    heads_part = H // members
     width_part = D // members
-    score_scale = DH ** (-0.5)
-    axis_hot = offset_table()
     vectors, fc_bias, rel_tables, special = unpack_small(small_params)
 
     blocks = []
     count_here = jnp.full((8, 128), jnp.sum(masked_count).astype(f4))
+    part = 2 * DH
     for l in range(LAYERS):
+        wq, wk, wv, wo = qkv_weight[l, 0], qkv_weight[l, 1], qkv_weight[l, 2], out_weight[l].T
         blocks.append(
             jnp.concatenate(
-                [qkv_weight[l, 0], qkv_weight[l, 1], qkv_weight[l, 2], out_weight[l].T], 1
+                [wq[:, :part], wk[:, :part], wv[:, :part], wq[:, part:], wv[:, part:],
+                 wk[:, part:], wo[:, part:], wo[:, :part]],
+                1,
             ).astype(bf)
         )
         blocks.append(up_weight[l].astype(bf))
@@ -762,196 +1274,117 @@
     hidden_patch = jnp.any(
         (masked_spots[:, :, None] == jnp.arange(PATCH)[None, None, :]) & valid_slots[:, :, None], 1
     )
-    masked_rows = jnp.concatenate([jnp.zeros((images, 1), jnp.bool_), hidden_patch], 1).reshape(-1)
-    cls_rows = jnp.arange(rows_all) % SEQ == 0
-    seen_rows = jnp.logical_not(masked_rows | cls_rows)
-    row_codes = jnp.concatenate([jnp.zeros((images, 1), jnp.int32), image_codes], 1).reshape(-1)
-    code_hot = (seen_rows[:, None] & (row_codes[:, None] == jnp.arange(V)[None, :])).astype(bf)
-    pick_hot = (masked_spots[:, :, None] + 1 == jnp.arange(SEQ)[None, None, :]).astype(f4)
-    targets = jnp.take_along_axis(image_codes, masked_spots, 1).reshape(-1)
-    valid_float = valid_slots.reshape(-1).astype(f4)
+    token = jnp.arange(IMG)[None, :]
+
+    def by_token(values, fill):
+        return jnp.pad(values, ((0, 0), (1, IMG - SEQ)), constant_values=fill)
+
+    masked_rows = by_token(hidden_patch, False)
+    seen_rows = by_token(jnp.logical_not(hidden_patch), False)
+    kind = jnp.where(seen_rows, 0, jnp.where(token == 0, 1, 2)).astype(jnp.int32).reshape(-1, 1)
+    codes = jnp.where(seen_rows, by_token(image_codes, -1), -1).reshape(-1, 1)
+    slot_pad = ((0, 0), (0, -MAXM % 16))
+    targets = jnp.sum(
+        jnp.where(
+            masked_spots[:, :, None] == jnp.arange(PATCH)[None, None, :], image_codes[:, None, :], 0
+        ),
+        2,
+    )
+    targets = jnp.pad(targets, slot_pad, constant_values=-1).reshape(-1, 1)
+    spots = jnp.pad(masked_spots + 1, slot_pad, constant_values=-1).reshape(-1, 1)
+    valid_float = jnp.pad(valid_slots.astype(f4), slot_pad).reshape(-1, 1)
     row_weight = valid_float * inverse_total
 
-    def by_rows(x, w):
-        return lax.dot_general(x, w, (((1,), (1,)), ((), ())), preferred_element_type=f4)
-
-    def dot(x, w):
-        return jnp.dot(x, w, preferred_element_type=f4)
-
-    def split_heads(values):
-        return values.reshape(images, SEQ, H, DH)
-
-    def out_part(attn_mat):
-        return attn_mat.reshape(D, members, 4 * width_part)[:, :, 3 * width_part :].reshape(D, D)
-
-    embedded = by_rows(code_hot, table)
-    fallback = jnp.where(cls_rows[:, None], special[0], special[1])
-    x = jnp.where(seen_rows[:, None], embedded, fallback)
-    caches = []
+    biases = rel_biases(rel_tables).reshape(LAYERS, H, IMG, IMG)
+    x = embed(codes, kind, special, table, members, images)
+    kept = []
     for l in range(LAYERS):
-        attn_mat, up_mat, down_mat = layer_mats[l]
         vec = vectors[l]
-        attn_in = layer_norm(x, vec[0], vec[1]).astype(bf)
-        projected = dot(attn_in, attn_mat).reshape(rows_all, members, 4, width_part)
-        query_rows = (projected[:, :, 0].reshape(rows_all, D) + vec[2]).astype(bf)
-        key_rows = projected[:, :, 1].reshape(rows_all, D).astype(bf)
-        value_rows = (projected[:, :, 2].reshape(rows_all, D) + vec[3]).astype(bf)
-        rel_bias = bias_block(rel_tables[l], axis_hot)
-        raw_scores = jnp.einsum(
-            "bqhd,bkhd->bhqk", split_heads(query_rows), split_heads(key_rows),
-            preferred_element_type=f4,
+        bias_q = vec[2].reshape(members, width_part)
+        bias_v = vec[3].reshape(members, width_part)
+        zeros = jnp.zeros((members, part), f4)
+        proj_bias = jnp.concatenate(
+            [bias_q[:, :part], zeros, bias_v[:, :part], bias_q[:, part:], bias_v[:, part:], zeros, zeros],
+            1,
+        ).reshape(1, 4 * D)
+        following, proj, mixed, attn_out, mid, mlp_in, pre, act, mlp = forward_layer(
+            x, vec, fc_bias[l][None], proj_bias, biases[l], layer_mats[l], members, images
         )
-        attn_probs = softmax_rows(raw_scores * score_scale + rel_bias[None])
-        mixed = (
-            jnp.einsum(
-                "bhqk,bkhd->bqhd", attn_probs.astype(bf), split_heads(value_rows),
-                preferred_element_type=f4,
-            )
-            .reshape(rows_all, D)
-            .astype(bf)
+        kept.append((x, mixed, act, (proj, mixed, attn_out, mid, mlp_in, pre, mlp)))
+        x = following
+    loss_tile, upstream, d_gain, d_shift, picked, picked_t, d_logits = head_and_loss(
+        x, special, spots, targets, row_weight, valid_float, table, images
+    )
+    loss_part = loss_tile[0, 0]
+    lefts, rights, arrays = [], [], []
+    vec_grads, fc_grads, sums = [None] * LAYERS, [None] * LAYERS, [None] * LAYERS
+
+    def cuts_of(width, size, parts):
+        return [
+            (first, size, tuple((left, right, first, width) for left, right in parts))
+            for first in range(0, width, size)
+        ]
+
+    for l in reversed(range(LAYERS)):
+        x_in, mixed, act, rest = kept[l]
+        (upstream, vec_grad, fc_grad, proj_grad, sums[l], d_pre, d_cat,
+         attn_in_t, g_attn_t, mlp_in_t, g_mlp_t) = backward_layer(
+            upstream, x_in, vectors[l], biases[l], rest, layer_mats[l], members, images
         )
-        out_mat = out_part(attn_mat)
-        attn_out = by_rows(mixed, out_mat) + vec[4]
-        x_mid = x + vec[5] * attn_out
-        mlp_in = layer_norm(x_mid, vec[6], vec[7]).astype(bf)
-        pre_act = dot(mlp_in, up_mat) + fc_bias[l]
-        activated = exact_gelu(pre_act).astype(bf)
-        mlp_out = by_rows(activated, down_mat) + vec[8]
-        caches.append(
-            (x, attn_in, query_rows, key_rows, value_rows, attn_probs, mixed, out_mat, attn_out,
-             x_mid, mlp_in, pre_act, activated, mlp_out)
+        proj_grad = proj_grad.reshape(members, 6 * TILE)
+        d_bias_q = jnp.concatenate([proj_grad[:, :part], proj_grad[:, 3 * part : 3 * part + DH]], 1)
+        d_bias_v = jnp.concatenate(
+            [proj_grad[:, 2 * part : 3 * part], proj_grad[:, 3 * part + DH : 4 * part]], 1
         )
-        x = x_mid + vec[9] * mlp_out
-
-    last_normed = layer_norm(x, special[2], special[3]).astype(bf)
-    picked = (
-        jnp.einsum(
-            "bst,btd->bsd", pick_hot.astype(bf), last_normed.reshape(images, SEQ, D),
-            preferred_element_type=f4,
+        vec_grads[l] = jnp.concatenate(
+            [vec_grad[:2], d_bias_q.reshape(1, D), d_bias_v.reshape(1, D), vec_grad[4:]], 0
         )
-        .astype(bf)
-        .reshape(images * MAXM, D)
-    )
-    logits = dot(picked, table)
-    target_hits = jnp.arange(V)[None, :] == targets[:, None]
-    target_logit = jnp.sum(jnp.where(target_hits, logits, 0.0), 1)
-    highest = jnp.max(logits, 1)
-    exp_sums = jnp.sum(jnp.exp(logits - highest[:, None]), 1)
-    log_total = highest + jnp.log(exp_sums)
-    loss_part = jnp.sum((log_total - target_logit) * valid_float)
-    d_logits = (
-        (jnp.exp(logits - log_total[:, None]) - target_hits.astype(f4)) * row_weight[:, None]
-    ).astype(bf)
-    d_picked = by_rows(d_logits, table)
-    d_normed = jnp.einsum(
-        "bst,bsd->btd", pick_hot, d_picked.reshape(images, MAXM, D), precision=HIGHEST
-    ).reshape(rows_all, D)
-    unused, pullback = jax.vjp(layer_norm, x, special[2], special[3])
-    upstream, d_gain, d_shift = pullback(d_normed)
-
-    def padded(values):
-        return jnp.pad(values, ((0, depth - rows_all), (0, 0)))
-
-    pairs = [None] * LAYERS
-    vec_grads, fc_grads, rel_grads = [None] * LAYERS, [None] * LAYERS, [None] * LAYERS
-    for l in reversed(range(LAYERS)):
-        attn_mat, up_mat, down_mat = layer_mats[l]
-        (x_in, attn_in, query_rows, key_rows, value_rows, attn_probs, mixed, out_mat, attn_out,
-         x_mid, mlp_in, pre_act, activated, mlp_out) = caches[l]
-        vec = vectors[l]
-        g_mlp = (vec[9] * upstream).astype(bf)
-        d_gamma2 = jnp.sum(upstream * mlp_out, 0)
-        d_down_bias = jnp.sum(g_mlp.astype(f4), 0)
-        d_act = dot(g_mlp, down_mat)
-        unused, pullback = jax.vjp(exact_gelu, pre_act)
-        d_pre = pullback(d_act)[0].astype(bf)
-        fc_grads[l] = jnp.sum(d_pre.astype(f4), 0)
-        d_norm2 = by_rows(d_pre, up_mat)
-        unused, pullback = jax.vjp(layer_norm, x_mid, vec[6], vec[7])
-        d_mid, d_gain2, d_shift2 = pullback(d_norm2)
-        d_mid = d_mid + upstream
-        g_attn = (vec[5] * d_mid).astype(bf)
-        d_gamma1 = jnp.sum(d_mid * attn_out, 0)
-        d_out_bias = jnp.sum(g_attn.astype(f4), 0)
-        d_mixed = split_heads(dot(g_attn, out_mat).astype(bf))
-        d_probs = jnp.einsum(
-            "bqhd,bkhd->bhqk", d_mixed, split_heads(value_rows), preferred_element_type=f4
-        )
-        d_value = jnp.einsum(
-            "bhqk,bqhd->bkhd", attn_probs.astype(bf), d_mixed, preferred_element_type=f4
-        ).astype(bf)
-        d_scores = (
-            attn_probs * (d_probs - jnp.sum(attn_probs * d_probs, -1, keepdims=True))
-        ).astype(bf)
-        d_query = (
-            jnp.einsum(
-                "bhqk,bkhd->bqhd", d_scores, split_heads(key_rows), preferred_element_type=f4
-            )
-            * score_scale
-        ).astype(bf)
-        d_key = (
-            jnp.einsum(
-                "bhqk,bqhd->bkhd", d_scores, split_heads(query_rows), preferred_element_type=f4
-            )
-            * score_scale
-        ).astype(bf)
-        rel_grads[l] = bias_grad(jnp.sum(d_scores.astype(f4), 0), axis_hot)
-
-        def parts(values):
-            return values.reshape(rows_all, members, 1, width_part)
-
-        d_cat = jnp.concatenate(
-            [parts(d_query), parts(d_key), parts(d_value), jnp.zeros_like(parts(d_value))], 2
-        ).reshape(rows_all, 4 * D)
-        mixed_cat = jnp.pad(parts(mixed), ((0, 0), (0, 0), (3, 0), (0, 0))).reshape(rows_all, 4 * D)
-        d_norm1 = by_rows(d_cat, attn_mat)
-        unused, pullback = jax.vjp(layer_norm, x_in, vec[0], vec[1])
-        d_input, d_gain1, d_shift1 = pullback(d_norm1)
-        vec_grads[l] = jnp.stack(
-            [
-                d_gain1, d_shift1,
-                jnp.sum(d_query.reshape(rows_all, D).astype(f4), 0),
-                jnp.sum(d_value.reshape(rows_all, D).astype(f4), 0),
-                d_out_bias, d_gamma1, d_gain2, d_shift2, d_down_bias, d_gamma2,
-            ]
-        )
-        pairs[l] = [
-            (
-                jnp.concatenate([padded(attn_in), padded(g_attn)], 0),
-                jnp.concatenate([padded(d_cat), padded(mixed_cat)], 0),
-            ),
-            (padded(mlp_in), padded(d_pre)),
-            (padded(g_mlp), padded(activated)),
+        fc_grads[l] = fc_grad[0]
+        i, j = len(lefts), len(rights)
+        lefts += [attn_in_t, g_attn_t, mlp_in_t, g_mlp_t]
+        rights += [d_cat, mixed, d_pre, act]
+        arrays += [
+            (D, [(0, 512, ((i, j, 0, D),)), (512, 256, ((i, j, 512, D), (i + 1, j + 1, 0, 256)))]),
+            (D, cuts_of(D, 384, ((i + 2, j + 2),))),
+            (D, cuts_of(D, 384, ((i + 3, j + 3),))),
         ]
-        upstream = d_input + d_mid
-    d_cls = jnp.sum(jnp.where(cls_rows[:, None], upstream, 0.0), 0)
-    d_mask = jnp.sum(jnp.where(masked_rows[:, None], upstream, 0.0), 0)
-    seen_grad = jnp.where(seen_rows[:, None], upstream, 0.0).astype(bf)
-    table_depth = images * MAXM + rows_all
-    table_pad = ((0, -table_depth % 16), (0, 0))
-    table_pair = (
-        jnp.pad(jnp.concatenate([picked, seen_grad], 0), table_pad),
-        jnp.pad(jnp.concatenate([d_logits, code_hot], 0), table_pad),
-    )
+    cls_rows = jnp.broadcast_to(token == 0, (images, IMG)).reshape(-1, 1)
+    d_cls = jnp.sum(jnp.where(cls_rows, upstream, 0.0), 0)
+    d_mask = jnp.sum(jnp.where(masked_rows.reshape(-1, 1), upstream, 0.0), 0)
+    seen_grad = jnp.where(seen_rows.reshape(-1, 1), upstream, 0.0).astype(bf)
+    i = len(lefts)
+    lefts += [picked_t, seen_grad.T]
+    arrays.append((V // members, cuts_of(V // members, 512, ((i, len(rights)), (i + 1, None)))))
+    rights.append(d_logits)
     small_grad = pack_small(
-        jnp.stack(vec_grads), jnp.stack(fc_grads), jnp.stack(rel_grads),
-        jnp.stack([d_cls, d_mask, d_gain, d_shift]),
+        jnp.stack(vec_grads), jnp.stack(fc_grads),
+        rel_grads(jnp.concatenate(sums, 0)),
+        jnp.stack([d_cls, d_mask, d_gain[0], d_shift[0]]),
     )
     small_size = small_grad.shape[0]
     packed = jnp.concatenate([small_grad, loss_part[None]])
     packed = jnp.pad(packed, (0, -packed.shape[0] % 1024)).reshape(-1, 128)
 
-    all_pairs = [table_pair] + [pair for l in reversed(range(LAYERS)) for pair in pairs[l]]
-    grads, small_sum, squares = reduce_products(all_pairs, packed, ndp, members)
-    grad_table = grads[0].T
-    by_layer = [grads[1 + 3 * (LAYERS - 1 - l) :][:3] for l in range(LAYERS)]
+    grads, small_sum, squares = reduce_products(lefts, rights, codes, arrays, packed, ndp, members)
+    grad_table = grads[-1].T
+    by_layer = [grads[3 * (LAYERS - 1 - l) :][:3] for l in range(LAYERS)]
+
+    def joined(g, first, second):
+        return jnp.concatenate([g[:, first : first + part], g[:, second : second + DH]], 1)
+
     grad_qkv = jnp.stack(
         [
-            jnp.stack([g[0][:, j * width_part : (j + 1) * width_part] for j in range(3)])
+            jnp.stack(
+                [
+                    joined(g[0], 0, 3 * part),
+                    joined(g[0], part, 4 * part),
+                    joined(g[0], 2 * part, 3 * part + DH),
+                ]
+            )
             for g in by_layer
         ]
     )
-    grad_out = jnp.stack([g[0][:, 3 * width_part :].T for g in by_layer])
+    grad_out = jnp.stack([joined(g[0], 5 * part, 4 * part + DH).T for g in by_layer])
     grad_up = jnp.stack([g[1] for g in by_layer])
     grad_down = jnp.stack([g[2].T for g in by_layer])
     small_sum = small_sum.reshape(-1)

time: 1150 us -> 775 us (0.67)
  local copies, waits for them, and re-layouts: 315 us -> 37.8 us
  matrix products: 199 us -> 0 us
  Pallas kernels: 503 us -> 698 us
  other arithmetic: 114 us -> 30 us
    pallas_call x0 -> x8, Pallas kernels: none -> 199 us  [the longest x2 77.2 us: backward_layer(): pl.pallas_call(functools.partial(backward_kernel, members, images), out_s...]
    dot_general x41 -> x0, matrix products: 199 us -> none  [the longest x9 69.4 us: dot(): return jnp.dot(x, w, preferred_element_type=f4)]
    reshape x41 -> x12, local copies, waits for them, and re-layouts: 105 us -> 5.15 us  [the longest x1 0.89 us: local(): codes = jnp.where(seen_rows, by_token(image_codes, -1), -1).reshape(-1, 1)]
    transpose x17 -> x1, local copies, waits for them, and re-layouts: 32.5 us -> 1.17 us  [local(): lefts += [picked_t, seen_grad.T]]
    another operation x30 -> x12, local copies, waits for them, and re-layouts: 32.8 us -> 1.87 us  [the longest x2 19.5 us: out_part(): attn_mat.reshape(D, members, 4 * width_part)[:, :, 3 * width_part:]]
    concatenate x8 -> x4, other arithmetic: 32.6 us -> 5.95 us  [the longest x1 5.15 us: local(): jnp.concatenate(sums, 0)]
    unnamed x373 -> x91, local copies, waits for them, and re-layouts: 36.2 us -> 9.82 us
    reduce_sum x27 -> x2, other arithmetic: 26.9 us -> 3.01 us  [the longest x1 1.57 us: local(): d_cls = jnp.sum(jnp.where(cls_rows, upstream, 0.0), 0)]
where the time goes in v2:
time: 775 us; the launch traced here: 771 us
  Pallas kernels  698 us (90%)
  local copies, waits for them, and re-layouts  37.8 us (5%)
  other arithmetic  30 us (4%)
    pallas_call x1, Pallas kernels, reduce_products(): pl.pallas_call(functools.partial(reduce_kernel, outer, inner, members, ro...  278 us
    pallas_call x1, Pallas kernels, gather_blocks(): pl.pallas_call(functools.partial(gather_kernel, outer, inner, members, gr...  220 us
    pallas_call x2, Pallas kernels, backward_layer(): pl.pallas_call(functools.partial(backward_kernel, members, images), out_s...  77.2 us
    pallas_call x2, Pallas kernels, forward_layer(): pl.pallas_call(functools.partial(forward_kernel, members, images), out_sh...  49 us
    pallas_call x1, Pallas kernels, rel_grads(): pl.pallas_call(rel_grad_kernel, grid=(number,), in_specs=[pl.BlockSpec((1...  23.8 us
    pallas_call x1, Pallas kernels, rel_biases(): pl.pallas_call(bias_kernel, grid=(number,), in_specs=[pl.BlockSpec((1, 1,...  21.8 us

profile of v2, /device:TPU:0, one launch (start us, length us, event | category | flops | bytes accessed | tf_op | source)
XLA Modules:
  0.0 771.1 jit_solution(7176823247986536481)
XLA Ops:
  0.7 1.3 fusion.13
  2.0 1.1 copy.76
  3.2 0.8 concatenate.66.refs_4_
  4.1 0.8 concatenate.65.refs_0_
  4.9 0.7 slice_bitcast_fusion
  5.7 0.7 slice_bitcast_fusion.1
  6.4 0.8 convert_bitcast_fusion.refs_1_
  9.1 220.2 %gather_blocks.1 = (bf16[2,2,2,96,3072]{4,3,2,1,0:T(8,128)(2,1)}, bf16[2,2,2,96,8192]{4,3,2,1,0:T(8,128)(2,1)}, bf16[2,2,2,96,3072]{4,3,2,1,0:T(8,128)(2,1)}, bf...) custom-call(bf16[96,768]{1,0:T(8,128)(2,1)} %concatenate.65.refs_0_,, ...), custom_call_target="tpu_custom_call" | custom-call | tf_op jit(solution)/shard_map/gather_blocks/pallas_call | solution.py:745
  230.8 0.9 reshape.281.codes_ref.refs_1_
  231.7 0.9 reshape.282.kind_ref
  233.8 12.0 %embed.1.x_ref = f32[416,768]{1,0:T(8,128)} custom-call(s32[416,1]{1,0:T(8,128)} %reshape.281.codes_ref.refs_1_, s32[416,1]{1,0:T(8,128)} %reshape.282.kind_ref, f32[4,768]{1,0:T(4,128)} %reshape.232.special_ref, bf16[768,8192]{1,0:T(8,128)(2,1)} %bitcast.122), custom_call_target="tpu_custom_call" | custom-call | tf_op jit(solution)/shard_map/embed/pallas_call | solution.py:516
  246.8 0.8 reverse
  249.3 21.8 %rel_biases.1 = f32[24,208,208]{2,1,0:T(8,128)} custom-call(f32[24,1,768]{2,1,0:T(1,128)} %pad.37.rel_ref, f32[24,1,128]{2,1,0:T(1,128)} %pad.38.extra_ref), custom_call_target="tpu_custom_call" | custom-call | tf_op jit(solution)/shard_map/rel_biases/pallas_call | solution.py:153
  271.1 5.2 fusion.23
  276.9 24.4 %forward_layer.2 = (f32[416,768]{1,0:T(8,128)}, bf16[4,416,640]{2,1,0:T(8,128)(2,1)}, bf16[4,416,256]{2,1,0:T(8,128)(2,1)}, f32[416,768]{1,0:T(8,128)}, f32[416,...) custom-call(f32[416,768]{1,0:T(8,128)} %embed.1.x_ref, ...), custom_call_target="tpu_custom_call" | custom-call | tf_op jit(solution)/shard_map/forward_layer/pallas_call | solution.py:530
  302.8 24.6 %forward_layer.3 = (f32[416,768]{1,0:T(8,128)}, bf16[4,416,640]{2,1,0:T(8,128)(2,1)}, bf16[4,416,256]{2,1,0:T(8,128)(2,1)}, f32[416,768]{1,0:T(8,128)}, f32[416,...) custom-call(f32[416,768]{1,0:T(8,128)} %get-tuple-element.90.x_ref, ...), custom_call_target="tpu_custom_call" | custom-call | tf_op jit(solution)/shard_map/forward_layer/pallas_call | solution.py:530
  327.4 1.4 slice_reduce_fusion
  329.4 0.8 reshape.285.weight_ref
  330.2 1.4 select_reduce_fusion.2
  331.8 0.8 reshape.284.targets_ref
  332.6 0.8 reshape.286.valid_ref
  333.4 0.8 reshape.283.spots_ref
  334.2 15.4 %head_and_loss.1 = (f32[8,128]{1,0:T(8,128)}, f32[416,768]{1,0:T(8,128)}, f32[1,768]{1,0:T(1,128)}, f32[1,768]{1,0:T(1,128)}, bf16[160,768]{1,0:T(8,128)(2,1)}, ...) custom-call(f32[416,768]{1,0:T(8,128)} %get-tuple-element.94.x_ref, f32[4,768]{1,0:T(4,128)} %reshape.232.special_ref, ...), custom_call_target="tpu_custom_call" | custom-call | tf_op jit(solution)/shard_map/head_and_loss/pallas_call | solution.py:555
  349.6 38.7 %backward_layer.2 = (f32[416,768]{1,0:T(8,128)}, f32[10,768]{1,0:T(8,128)}, f32[1,3072]{1,0:T(1,128)}, f32[1,3072]{1,0:T(1,128)}, f32[12,208,208]{2,1,0:T(8,128)...) custom-call(f32[416,768]{1,0:T(8,128)} %get-tuple-element.96.up_ref,, ...), custom_call_target="tpu_custom_call" | custom-call | tf_op jit(solution)/shard_map/backward_layer/pallas_call | solution.py:584
  388.4 38.5 %backward_layer.3 = (f32[416,768]{1,0:T(8,128)}, f32[10,768]{1,0:T(8,128)}, f32[1,3072]{1,0:T(1,128)}, f32[1,3072]{1,0:T(1,128)}, f32[12,208,208]{2,1,0:T(8,128)...) custom-call(f32[416,768]{1,0:T(8,128)} %get-tuple-element.104.up_ref, ...), custom_call_target="tpu_custom_call" | custom-call | tf_op jit(solution)/shard_map/backward_layer/pallas_call | solution.py:584
  427.2 1.6 select_reduce_fusion.1
  428.8 5.1 pad_maximum_fusion.sums_ref
  434.0 23.8 %rel_grads.1 = (f32[24,1,768]{2,1,0:T(1,128)}, f32[24,1,128]{2,1,0:T(1,128)}) custom-call(f32[24,208,208]{2,1,0:T(8,128)} %pad_maximum_fusion.sums_ref), custom_call_target="tpu_custom_call" | custom-call | tf_op jit(solution)/shard_map/rel_grads/pallas_call | solution.py:199
  457.9 2.6 reverse.1
  460.7 0.8 pad_maximum_fusion.2
  464.3 1.2 slice.367
  465.5 0.7 concatenate.77
  467.2 1.2 copy.87
  468.4 278.2 %reduce_products.1 = (f32[96,768]{1,0:T(8,128)}, f32[96,768]{1,0:T(8,128)}, f32[96,768]{1,0:T(8,128)}, f32[96,768]{1,0:T(8,128)}, f32[96,768]{1,0:T(8,128)}, /*i...) custom-call(f32[336,128]{1,0:T(8,128)} %pad_bitcast_fusion.refs_0_, ...), custom_call_target="tpu_custom_call" | custom-call | tf_op jit(solution)/shard_map/reduce_products/pallas_call | solution.py:1211
  746.6 1.6 multiply_reduce_fusion
  748.2 1.3 reduce_sum.68
  750.9 1.8 multiply_subtract_fusion.5
  752.7 3.6 multiply_subtract_fusion
  756.4 1.5 multiply_subtract_fusion.1
  758.5 1.5 multiply_subtract_fusion.2
  761.9 0.8 copy.93
  762.7 0.8 copy.94
  763.5 0.8 copy.95
  764.4 0.8 maximum_bitcast_fusion.2
  765.2 0.8 maximum_bitcast_fusion.3
  766.0 0.8 maximum_bitcast_fusion.5
  766.9 1.5 multiply_subtract_fusion.3
  768.5 1.3 slice.430
  (198 shorter events, 15.7 us)
Async XLA Ops:
  0.7 230.0 %copy-start = (s32[8,196]{1,0:T(8,128)S(1)}, s32[8,196]{1,0:T(8,128)}, u32[]{:S(2)}) copy-start(s32[8,196]{1,0:T(8,128)} %param.39) | copy-start | bytes 18820
  0.7 4.2 copy-start.4
  0.7 4.9 copy-start.5
  2.0 4.4 copy-start.3
  3.2 4.0 copy-start.8
  3.2 4.0 copy-start.37
  4.9 227.7 %copy-start.10 = (f32[42144]{0:T(1024)S(1)}, f32[42144]{0:T(1024)}, u32[]{:S(2)}) copy-start(f32[42144]{0:T(1024)} %param.36) | copy-start | bytes 505732
  233.8 12.9 %slice-start = ((f32[42144]{0:T(1024)}), f32[17568]{0:T(1024)S(1)}, s32[]{:S(2)}) async-start(f32[42144]{0:T(1024)} %param.36), calls=%async_computation | async-start | bytes 147456 | tf_op jit(solution)/shard_map/slice | solution.py:40
  388.3 40.4 %copy-start.35 = (f32[1,768]{1,0:T(1,128)S(1)}, f32[1,768]{1,0:T(1,128)}, u32[]{:S(2)}) copy-start(f32[1,768]{1,0:T(1,128)} %get-tuple-element.123) | copy-start | bytes 9220
  388.4 40.4 %copy-start.36 = (f32[1,768]{1,0:T(1,128)S(1)}, f32[1,768]{1,0:T(1,128)}, u32[]{:S(2)}) copy-start(f32[1,768]{1,0:T(1,128)} %get-tuple-element.124) | copy-start | bytes 9220
  434.0 27.6 %copy-start.33 = (f32[1,3072]{1,0:T(1,128)S(1)}, f32[1,3072]{1,0:T(1,128)}, u32[]{:S(2)}) copy-start(f32[1,3072]{1,0:T(1,128)} %get-tuple-element.117) | copy-start | bytes 36868
  434.0 27.7 %copy-start.34 = (f32[1,3072]{1,0:T(1,128)S(1)}, f32[1,3072]{1,0:T(1,128)}, u32[]{:S(2)}) copy-start(f32[1,3072]{1,0:T(1,128)} %get-tuple-element.116) | copy-start | bytes 36868
  434.0 28.2 %copy-start.32 = (f32[1,3072]{1,0:T(1,128)S(1)}, f32[1,3072]{1,0:T(1,128)}, u32[]{:S(2)}) copy-start(f32[1,3072]{1,0:T(1,128)} %get-tuple-element.113) | copy-start | bytes 36868
  434.0 29.2 %copy-start.30 = (f32[10,768]{1,0:T(8,128)S(1)}, f32[10,768]{1,0:T(8,128)}, u32[]{:S(2)}) copy-start(f32[10,768]{1,0:T(8,128)} %get-tuple-element.112) | copy-start | bytes 92164
  434.0 29.2 %copy-start.31 = (f32[1,3072]{1,0:T(1,128)S(1)}, f32[1,3072]{1,0:T(1,128)}, u32[]{:S(2)}) copy-start(f32[1,3072]{1,0:T(1,128)} %get-tuple-element.115) | copy-start | bytes 36868
  434.0 30.2 %copy-start.29 = (f32[10,768]{1,0:T(8,128)S(1)}, f32[10,768]{1,0:T(8,128)}, u32[]{:S(2)}) copy-start(f32[10,768]{1,0:T(8,128)} %get-tuple-element.114) | copy-start | bytes 92164
  434.0 33.0 %copy-start.2 = (f32[416,768]{1,0:T(8,128)S(1)}, f32[416,768]{1,0:T(8,128)}, u32[]{:S(2)}) copy-start(f32[416,768]{1,0:T(8,128)} %get-tuple-element.122) | copy-start | bytes 3833860
  468.4 282.5 %copy-start.11 = (f32[42144]{0:T(1024)S(1)}, f32[42144]{0:T(1024)}, u32[]{:S(2)}) copy-start(f32[42144]{0:T(1024)} %param.36) | copy-start | bytes 505732
  468.4 282.5 %copy-start.27 = (f32[42144]{0:T(1024)S(1)}, f32[42144]{0:T(1024)}, u32[]{:S(2)}) copy-start(f32[42144]{0:T(1024)} %param.37) | copy-start | bytes 505732
  468.4 282.5 %copy-start.28 = (f32[42144]{0:T(1024)S(1)}, f32[42144]{0:T(1024)}, u32[]{:S(2)}) copy-start(f32[42144]{0:T(1024)} %param.38) | copy-start | bytes 505732
  752.7 3.6 copy-start.12
  752.7 3.6 copy-start.13
  752.7 3.6 copy-start.22
  752.7 3.7 copy-start.23
  756.3 1.6 copy-start.6
  756.3 1.6 copy-start.14
  756.3 2.0 copy-start.15
  756.3 2.1 copy-start.20
  756.3 2.2 copy-start.21
  757.9 2.2 copy-start.19
  758.5 2.2 copy-start.18
  758.5 2.9 copy-start.24
  758.5 3.0 copy-start.25
  758.5 3.2 copy-start.9
  761.7 5.2 copy-start.7
  761.7 5.2 copy-start.16
  761.7 5.2 copy-start.17
  761.9 4.9 copy-start.26
  766.8 2.9 copy-start.1
